TPU v7x, 256 devices: a whole 4x4x8 slice. The times are simulated.
256 devices in a mesh: rep: 32 (over z, y_lo, core), fsdp: 8 (over y_hi, x).
Axes of the slice: x: 4, y: 4 (y_hi: 2, y_lo: 2; y = y_hi * 2 + y_lo), z: 8, core: 2. Of those that a mesh axis runs over, the one named last changes fastest.
Arguments:
- tokens: bfloat16 [32768, 1536], P(('rep', 'fsdp')), may hold values from -6 to 6
- segment_ids: int32 [32768], P('rep'), may hold values from 0 to 3, as said below
- routes: int32 [32768, 6], P(('rep', 'fsdp')), may hold values from 0 to 7, all different within a row
- gain_attn: bfloat16 [1536], P('fsdp'), may hold values from 0.099609375 to 1.8984375
- w_query: bfloat16 [1536, 1536], P('fsdp'), may hold values from -0.3125 to 0.3125
- w_key: bfloat16 [1536, 512], P('fsdp'), may hold values from -0.15625 to 0.15625
- w_value: bfloat16 [1536, 512], P('fsdp'), may hold values from -0.15625 to 0.15625
- w_out: bfloat16 [1536, 1536], P('fsdp'), may hold values from -0.625 to 0.625
- gain_ffn: bfloat16 [1536], P('fsdp'), may hold values from 0.099609375 to 1.8984375
- w_router: bfloat16 [1536, 8], P('fsdp'), may hold values from -0.078125 to 0.078125
- w_shared_in: bfloat16 [1536, 2048], P('fsdp'), may hold values from -0.15625 to 0.15625
- w_shared_out: bfloat16 [1024, 1536], P('fsdp'), may hold values from -0.375 to 0.375
- w_expert_in: bfloat16 [1536, 8, 1024], P('fsdp'), may hold values from -0.15625 to 0.15625
- w_expert_out: bfloat16 [8, 512, 1536], P(None, 'fsdp'), may hold values from -1 to 1
- cotangent: bfloat16 [32768, 1536], P(('rep', 'fsdp')), may hold values from -6 to 6
Outputs:
- result: bfloat16 [32768, 1536], P(('rep', 'fsdp'))
- grad_input: bfloat16 [32768, 1536], P(('rep', 'fsdp'))
- grad_gain_attn: float32 [1536], P('fsdp')
- grad_query: float32 [1536, 1536], P('fsdp')
- grad_key: float32 [1536, 512], P('fsdp')
- grad_value: float32 [1536, 512], P('fsdp')
- grad_out: float32 [1536, 1536], P('fsdp')
- grad_gain_ffn: float32 [1536], P('fsdp')
- grad_router: float32 [1536, 8], P('fsdp')
- grad_shared_in: float32 [1536, 2048], P('fsdp')
- grad_shared_out: float32 [1024, 1536], P('fsdp')
- grad_expert_in: float32 [1536, 8, 1024], P('fsdp')
- grad_expert_out: float32 [8, 512, 1536], P(None, 'fsdp')
Inputs may be any that keep to these rules, and one draw needn't show every extreme that they name: `segment_ids`: within each sequence of 1024 tokens, documents 1, 2, 3 follow one another and padding 0 closes the sequence; document 2 begins on the sequence's first device and ends on its last. `routes`: 6 different experts for each token.
All inputs are finite; a program needn't handle non-finite values.
Results may differ from a plain program's by a relative error of at most 0.03.
Values may be sent and summed in bfloat16 or wider, within the bound.
No kernel may reach another device: no remote copies, remote signals or barrier semaphores. Data moves between devices by JAX's collectives and lax.ppermute only.
A program may use at most 256 MiB of HBM per device.

v0:
```python
import math

import jax
import jax.numpy as jnp
from jax import lax
from jax.sharding import PartitionSpec as P

HEADS = 12
KV_HEADS = 4
HEAD = 128
FE = 512
FS = 1024


eps_norm = 1e-05


def side_by_side(arrays, axis, dim, along):
    widths = [math.prod(a.shape[along:]) for a in arrays]
    both = jnp.concatenate(
        [a.reshape(*a.shape[:along], w) for a, w in zip(arrays, widths)], axis=along
    )
    whole = lax.all_gather(both, axis, axis=dim, tiled=True)
    pieces = jnp.split(whole, [sum(widths[:k]) for k in range(1, len(widths))], axis=along)
    return tuple(
        (b.reshape(*whole.shape[:along], *a.shape[along:]) for a, b in zip(arrays, pieces))
    )


def side_by_side_2(arrays, axis, dim, along):
    ends, at = ([], 0)
    for a in arrays[:-1]:
        at += a.shape[along]
        ends.append(at)
    both = jnp.concatenate(arrays, axis=along)
    return tuple(jnp.split(lax.all_gather(both, axis, axis=dim, tiled=True), ends, axis=along))


def joined_along(pieces, dim):
    lengths = list(pieces.shape[1:])
    lengths[dim] *= pieces.shape[0]
    return jnp.moveaxis(pieces, 0, dim).reshape(lengths)


def gather_packed(arrays, axis, dims):
    flat = jnp.concatenate([a.reshape(-1) for a in arrays])
    lines, at, gathered = (lax.all_gather(flat, axis), 0, [])
    for a, dim in zip(arrays, dims):
        pieces = lines[:, at : at + a.size].reshape(-1, *a.shape)
        gathered.append(joined_along(pieces, dim))
        at += a.size
    return tuple(gathered)


def in_blocks(array, dim, length):
    before, after = (array.shape[:dim], array.shape[dim + 1 :])
    return jnp.moveaxis(array.reshape(*before, length, -1, *after), dim, 0)


def summed_on_arrival(array, axis, dim):
    length = lax.axis_size(axis)
    pieces = lax.all_to_all(in_blocks(array, dim, length), axis, 0, 0, tiled=True)
    return jnp.sum(pieces, axis=0)


def in_one_piece(arrays, axis, dim, along):
    widths = [a.shape[along] for a in arrays]
    both = jnp.concatenate(arrays, axis=along)
    whole = lax.psum_scatter(both, axis, scatter_dimension=dim, tiled=True)
    return tuple(jnp.split(whole, [sum(widths[:k]) for k in range(1, len(widths))], axis=along))


def sent_together(arrays, axis, dim, along):
    columns = [a.reshape(*a.shape[:along], -1) for a in arrays]
    both = jnp.concatenate(columns, axis=along)
    whole, at, gathered = (lax.psum_scatter(both, axis, scatter_dimension=dim, tiled=True), 0, [])
    for a, column in zip(arrays, columns):
        section = whole[..., at : at + column.shape[along]]
        gathered.append(section.reshape(*section.shape[:along], *a.shape[along:]))
        at += column.shape[along]
    return tuple(gathered)


def dot_rows(left, right):
    return lax.dot_general(
        left, right, (((1,), (1,)), ((), ())), preferred_element_type=jnp.float32
    )


def dot_cols(left, right):
    return lax.dot_general(
        left, right, (((0,), (0,)), ((), ())), preferred_element_type=jnp.float32
    )


def normalize(values):
    factor = lax.rsqrt(jnp.mean(values * values, axis=-1, keepdims=True) + eps_norm)
    return (values * factor, factor)


def norm_back(grad_normed, unit, factor, gain):
    scaled = grad_normed * gain
    gain_grad = jnp.sum(grad_normed * unit, axis=0)
    inner = jnp.mean(scaled * unit, axis=-1, keepdims=True)
    return (factor * (scaled - unit * inner), gain_grad)


def silu_slope(values, sig):
    return sig * (1.0 + values * (1.0 - sig))


def shards(
    tokens,
    segment_ids,
    routes,
    gain_attn,
    w_query,
    w_key,
    w_value,
    w_out,
    gain_ffn,
    w_router,
    w_shared_in,
    w_shared_out,
    w_expert_in,
    w_expert_out,
    cotangent,
):
    local_rows = tokens.shape[0]
    group_len = segment_ids.shape[0]
    per_group = HEADS // KV_HEADS
    qk_scale = 1.0 / math.sqrt(HEAD)
    experts_count = w_router.shape[1]
    start_row = lax.axis_index("fsdp") * local_rows
    seg_local = lax.dynamic_slice_in_dim(segment_ids, start_row, local_rows)
    query_pos = start_row + jnp.arange(local_rows, dtype=jnp.int32)
    key_pos = jnp.arange(group_len, dtype=jnp.int32)
    allowed = (query_pos[:, None] == key_pos[None, :]) | (key_pos[None, :] < query_pos[:, None]) & (
        seg_local[:, None] == segment_ids[None, :]
    ) & (segment_ids[None, :] != 0)
    inputs = tokens.astype(jnp.float32)
    attn_in = side_by_side((gain_attn, w_query, w_key, w_value), "fsdp", 0, 1)
    unit_one, factor_one = normalize(inputs)
    gain_one = attn_in[0].astype(jnp.float32)
    normed_one = (unit_one * gain_one).astype(jnp.bfloat16)
    query = jnp.dot(normed_one, attn_in[1], preferred_element_type=jnp.float32).astype(jnp.bfloat16)
    key_local = jnp.dot(normed_one, attn_in[2], preferred_element_type=jnp.float32).astype(
        jnp.bfloat16
    )
    value_local = jnp.dot(normed_one, attn_in[3], preferred_element_type=jnp.float32).astype(
        jnp.bfloat16
    )
    keys_all, values_all = side_by_side_2((key_local, value_local), "fsdp", 0, 1)
    query_heads = query.reshape(local_rows, KV_HEADS, per_group, HEAD)
    key_heads = keys_all.reshape(group_len, KV_HEADS, HEAD)
    value_heads = values_all.reshape(group_len, KV_HEADS, HEAD)

    def scores_of():
        raw = (
            jnp.einsum("tkgd,skd->kgts", query_heads, key_heads, preferred_element_type=jnp.float32)
            * qk_scale
        )
        return jnp.where(allowed[None, None], raw, -1e30)

    scores = scores_of()
    top_score = jnp.max(scores, axis=-1, keepdims=True)
    expo = jnp.exp(scores - top_score)
    total = jnp.sum(expo, axis=-1, keepdims=True)
    log_total = top_score + jnp.log(total)
    probs = (expo / total).astype(jnp.bfloat16)
    attended = jnp.einsum("kgts,skd->tkgd", probs, value_heads, preferred_element_type=jnp.float32)
    attended = attended.reshape(local_rows, HEADS * HEAD).astype(jnp.bfloat16)
    out_full = lax.all_gather(w_out, "fsdp", axis=0, tiled=True)
    hidden = inputs + jnp.dot(attended, out_full, preferred_element_type=jnp.float32)
    ffn_in = (
        lax.all_gather(gain_ffn, "fsdp", axis=0, tiled=True),
        lax.all_gather(w_router, "fsdp", axis=0, tiled=True),
        lax.all_gather(w_shared_in, "fsdp", axis=0, tiled=True),
        lax.all_gather(w_expert_in, "fsdp", axis=0, tiled=True),
    )
    unit_two, factor_two = normalize(hidden)
    gain_two = ffn_in[0].astype(jnp.float32)
    normed_two = (unit_two * gain_two).astype(jnp.bfloat16)
    logits = jnp.dot(normed_two, ffn_in[1], preferred_element_type=jnp.float32)
    chosen = jnp.sum(
        (routes[:, :, None] == jnp.arange(experts_count, dtype=jnp.int32)[None, None, :]).astype(
            jnp.float32
        ),
        axis=1,
    )
    weighted = chosen * jnp.exp(logits)
    gates = weighted / jnp.sum(weighted, axis=-1, keepdims=True)
    expert_pre = jnp.einsum(
        "td,def->tef", normed_two, ffn_in[3], preferred_element_type=jnp.float32
    )
    gate_part = expert_pre[:, :, :FE]
    up_part = expert_pre[:, :, FE:]
    gate_sig = jax.nn.sigmoid(gate_part)
    activ = gate_part * gate_sig * up_part
    mixed = (gates[:, :, None] * activ).astype(jnp.bfloat16)
    shared_pre = jnp.dot(normed_two, ffn_in[2], preferred_element_type=jnp.float32)
    shared_gate = shared_pre[:, :FS]
    shared_up = shared_pre[:, FS:]
    shared_sig = jax.nn.sigmoid(shared_gate)
    shared_act = (shared_gate * shared_sig * shared_up).astype(jnp.bfloat16)
    ffn_out = gather_packed((w_expert_out, w_shared_out), "fsdp", (1, 0))
    result = hidden + jnp.einsum(
        "tef,efd->td", mixed, ffn_out[0], preferred_element_type=jnp.float32
    )
    result = result + jnp.dot(shared_act, ffn_out[1], preferred_element_type=jnp.float32)
    grad_top = cotangent.astype(jnp.float32)
    grad_mixed = jnp.einsum(
        "td,efd->tef", cotangent, ffn_out[0], preferred_element_type=jnp.float32
    )
    grad_shared = dot_rows(cotangent, ffn_out[1])
    grad_gates = jnp.sum(grad_mixed * activ, axis=-1)
    grad_activ = grad_mixed * gates[:, :, None]
    grad_pre = jnp.concatenate(
        [grad_activ * up_part * silu_slope(gate_part, gate_sig), grad_activ * gate_part * gate_sig],
        axis=-1,
    ).astype(jnp.bfloat16)
    grad_logits = (
        gates * (grad_gates - jnp.sum(gates * grad_gates, axis=-1, keepdims=True))
    ).astype(jnp.bfloat16)
    grad_spre = jnp.concatenate(
        [
            grad_shared * shared_up * silu_slope(shared_gate, shared_sig),
            grad_shared * shared_gate * shared_sig,
        ],
        axis=-1,
    ).astype(jnp.bfloat16)
    router_back, shared_back, expert_back = (ffn_in[1], ffn_in[2], ffn_in[3])
    grad_normed_two = jnp.einsum(
        "tef,def->td", grad_pre, expert_back, preferred_element_type=jnp.float32
    )
    grad_normed_two = (
        grad_normed_two + dot_rows(grad_spre, shared_back) + dot_rows(grad_logits, router_back)
    )
    grad_norm_two, grad_gain_ffn = norm_back(grad_normed_two, unit_two, factor_two, gain_two)
    grad_hidden = grad_top + grad_norm_two
    width_own = w_router.shape[0]
    col_start = lax.axis_index("fsdp") * width_own
    fe_own = w_expert_out.shape[1]
    fe_start = lax.axis_index("fsdp") * fe_own
    fs_own = w_shared_out.shape[0]
    fs_start = lax.axis_index("fsdp") * fs_own
    pieces = side_by_side((normed_two, grad_pre, grad_spre, grad_logits), "fsdp", 0, 1)
    part_normed = lax.dynamic_slice_in_dim(pieces[0], col_start, width_own, 1)
    router_part = dot_cols(part_normed, pieces[3])
    shared_part = dot_cols(part_normed, pieces[2])
    expert_part = jnp.einsum(
        "td,tef->def", part_normed, pieces[1], preferred_element_type=jnp.float32
    )
    shared_in_own = shared_part
    expert_in_own = expert_part
    pieces = side_by_side((mixed, shared_act, cotangent), "fsdp", 0, 1)
    part_mixed = lax.dynamic_slice_in_dim(pieces[0], fe_start, fe_own, 2)
    part_shared = lax.dynamic_slice_in_dim(pieces[1], fs_start, fs_own, 1)
    expert_part = jnp.einsum(
        "tef,td->efd", part_mixed, pieces[2], preferred_element_type=jnp.float32
    )
    shared_part = dot_cols(part_shared, pieces[2])
    gain_own = summed_on_arrival(grad_gain_ffn, "fsdp", 0)
    ffn_owned = (gain_own, router_part, shared_in_own, expert_in_own, shared_part, expert_part)
    hidden_low = grad_hidden.astype(jnp.bfloat16)
    grad_out = dot_cols(attended, hidden_low)
    grad_att = dot_rows(hidden_low, out_full).astype(jnp.bfloat16)
    grad_heads = grad_att.reshape(local_rows, KV_HEADS, per_group, HEAD)
    probs_again = jnp.exp(scores_of() - log_total)
    grad_probs = jnp.einsum(
        "tkgd,skd->kgts", grad_heads, value_heads, preferred_element_type=jnp.float32
    )
    inner = jnp.sum(probs_again * grad_probs, axis=-1, keepdims=True)
    grad_scores = (probs_again * (grad_probs - inner)).astype(jnp.bfloat16)
    grad_query_rows = (
        jnp.einsum("kgts,skd->tkgd", grad_scores, key_heads, preferred_element_type=jnp.float32)
        * qk_scale
    )
    grad_query_rows = grad_query_rows.reshape(local_rows, HEADS * HEAD).astype(jnp.bfloat16)
    grad_keys_all = (
        jnp.einsum("kgts,tkgd->skd", grad_scores, query_heads, preferred_element_type=jnp.float32)
        * qk_scale
    )
    grad_values_all = jnp.einsum(
        "kgts,tkgd->skd",
        probs_again.astype(jnp.bfloat16),
        grad_heads,
        preferred_element_type=jnp.float32,
    )
    key_sum, value_sum = tuple(
        (
            part.astype(jnp.float32)
            for part in in_one_piece(
                (
                    grad_keys_all.reshape(group_len, KV_HEADS * HEAD).astype(jnp.bfloat16),
                    grad_values_all.reshape(group_len, KV_HEADS * HEAD).astype(jnp.bfloat16),
                ),
                "fsdp",
                0,
                1,
            )
        )
    )
    grad_key_rows = key_sum.astype(jnp.bfloat16)
    grad_value_rows = value_sum.astype(jnp.bfloat16)
    query_back, key_back, value_back = (attn_in[1], attn_in[2], attn_in[3])
    grad_normed_one = (
        dot_rows(grad_query_rows, query_back)
        + dot_rows(grad_key_rows, key_back)
        + dot_rows(grad_value_rows, value_back)
    )
    grad_query = dot_cols(normed_one, grad_query_rows)
    grad_key = dot_cols(normed_one, grad_key_rows)
    grad_value = dot_cols(normed_one, grad_value_rows)
    grad_norm_one, grad_gain_attn = norm_back(grad_normed_one, unit_one, factor_one, gain_one)
    grad_input = (grad_hidden + grad_norm_one).astype(jnp.bfloat16)
    attn_owned = tuple(
        (
            part.astype(jnp.float32)
            for part in sent_together(
                (
                    grad_gain_attn.astype(jnp.bfloat16),
                    grad_query.astype(jnp.bfloat16),
                    grad_key.astype(jnp.bfloat16),
                    grad_value.astype(jnp.bfloat16),
                    grad_out.astype(jnp.bfloat16),
                ),
                "fsdp",
                0,
                1,
            )
        )
    )
    summed = (
        lax.psum(attn_owned[0].astype(jnp.bfloat16), "rep").astype(jnp.float32),
        lax.psum(attn_owned[1].astype(jnp.bfloat16), "rep").astype(jnp.float32),
        lax.psum(attn_owned[2].astype(jnp.bfloat16), "rep").astype(jnp.float32),
        lax.psum(attn_owned[3].astype(jnp.bfloat16), "rep").astype(jnp.float32),
        lax.psum(attn_owned[4].astype(jnp.bfloat16), "rep").astype(jnp.float32),
        lax.psum(ffn_owned[0].astype(jnp.bfloat16), "rep").astype(jnp.float32),
        lax.psum(ffn_owned[1].astype(jnp.bfloat16), "rep").astype(jnp.float32),
        lax.psum(ffn_owned[2].astype(jnp.bfloat16), "rep").astype(jnp.float32),
        lax.psum(ffn_owned[4].astype(jnp.bfloat16), "rep").astype(jnp.float32),
        lax.psum(ffn_owned[3].astype(jnp.bfloat16), "rep").astype(jnp.float32),
        lax.psum(ffn_owned[5].astype(jnp.bfloat16), "rep").astype(jnp.float32),
    )
    return (
        result.astype(jnp.bfloat16),
        grad_input,
        summed[0],
        summed[1],
        summed[2],
        summed[3],
        summed[4],
        summed[5],
        summed[6],
        summed[7],
        summed[8],
        summed[9],
        summed[10],
    )


def solution(mesh):
    return jax.shard_map(
        shards,
        mesh=mesh,
        in_specs=(
            P(("rep", "fsdp"), None),
            P("rep"),
            P(("rep", "fsdp"), None),
            P("fsdp"),
            P("fsdp", None),
            P("fsdp", None),
            P("fsdp", None),
            P("fsdp", None),
            P("fsdp"),
            P("fsdp", None),
            P("fsdp", None),
            P("fsdp", None),
            P("fsdp", None, None),
            P(None, "fsdp", None),
            P(("rep", "fsdp"), None),
        ),
        out_specs=(
            P(("rep", "fsdp"), None),
            P(("rep", "fsdp"), None),
            P("fsdp"),
            P("fsdp", None),
            P("fsdp", None),
            P("fsdp", None),
            P("fsdp", None),
            P("fsdp"),
            P("fsdp", None),
            P("fsdp", None),
            P("fsdp", None),
            P("fsdp", None, None),
            P(None, "fsdp", None),
        ),
        check_vma=False,
    )
```

profile of v0, /device:TPU:1, one launch (start us, length us, event | category | flops | bytes accessed | tf_op | source)
XLA Modules:
  0.0 1895.2 jit_solution(13531483751671472540)
XLA Ops:
  10.9 116.5 %all-gather.11.cloned.1.call-done = bf16[1536,2561]{1,0:T(8,128)(2,1)} async-done(((bf16[192,2561]{1,0:T(8,128)(2,1)}), bf16[1536,2561]{1,0:T(8,128)(2,1)}) %all-gather.11.cloned.1.call-update) | async-done | bytes 7867408 | tf_op jit(solution)/shard_map/all_gather | solution.py:23
  148.5 16.4 all-reduce
  164.9 27.8 %all-gather.1 = bf16[8,192,8]{1,2,0:T(8,128)(2,1)S(1)} all-gather(bf16[1,192,8]{1,2,0:T(8,128)(2,1)S(1)} %bitcast.143), channel_id=1, replica_groups=mesh['rep'=32,'fsdp'=8] {'fsdp'}, dimensions={0}, use_global_device_ids=true | all-gather | bytes 27648 | tf_op jit(solution)/shard_map/all_gather | solution.py:177
  210.3 64.7 %all-gather.15.cloned.1.call-done = bf16[1536,1536]{1,0:T(8,128)(2,1)} async-done(((bf16[192,1536]{1,0:T(8,128)(2,1)}), bf16[1536,1536]{1,0:T(8,128)(2,1)}) %all-gather.15.cloned.1.call-update) | async-done | bytes 4718608 | tf_op jit(solution)/shard_map/all_gather | solution.py:173
  281.7 88.5 %all-gather.19.cloned.1.call-done = bf16[1536,2048]{1,0:T(8,128)(2,1)} async-done(((bf16[192,2048]{1,0:T(8,128)(2,1)}), bf16[1536,2048]{1,0:T(8,128)(2,1)}) %all-gather.19.cloned.1.call-update) | async-done | bytes 6291472 | tf_op jit(solution)/shard_map/all_gather | solution.py:178
  375.0 177.1 %all-gather.25.cloned.1.call-done = bf16[7864320]{0:T(1024)(128)(2,1)} async-done(((bf16[983040]{0:T(1024)(128)(2,1)}), bf16[7864320]{0:T(1024)(128)(2,1)}) %all-gather.25.cloned.1.call-update) | async-done | bytes 15728656 | tf_op jit(solution)/shard_map/all_gather | solution.py:47
  552.1 20.6 %reshape.239 = bf16[8,983040]{1,0:T(8,128)(2,1)} reshape(bf16[7864320]{0:T(1024)(128)(2,1)} %all-gather.25.cloned.1.call-done) | data formatting | bytes 31457280 | tf_op jit(solution)/shard_map/all_gather | solution.py:47
  572.7 10.8 slice.46
  586.6 13.2 copy.156
  602.1 219.0 %all-gather.17.cloned.1.call-done = bf16[1536,8,1024]{2,0,1:T(8,128)(2,1)} async-done(((bf16[192,8,1024]{2,0,1:T(8,128)(2,1)}), bf16[1536,8,1024]{2,0,1:T(8,128)(2,1)}) %all-gather.17.cloned.1.call-update) | async-done | bytes 25165840 | tf_op jit(solution)/shard_map/all_gather | solution.py:179
  821.1 10.0 fusion.78
  831.1 10.4 fusion.35
  853.2 13.6 convolution_bitcast_fusion.1
  913.3 56.2 %reduce-scatter.7.cloned.1.call-done = bf16[128,1024]{1,0:T(8,128)(2,1)} async-done(((bf16[1024,1024]{1,0:T(8,128)(2,1)}), bf16[128,1024]{1,0:T(8,128)(2,1)}) %reduce-scatter.7.cloned.1.call-update) | async-done | bytes 262160
  977.8 63.8 %concatenate.35 = bf16[1536,4097]{0,1:T(8,128)(2,1)} concatenate(bf16[1536,1]{0,1:T(2,128)(2,1)S(1)} %convert_element_type.236, bf16[1536,1536]{0,1:T(8,128)(2,1)} %convolution_convert_fusion, bf16[1536,512]{0,1:T(8,128)(2,1)S(1)} %convolution_convert_fusion.3, bf16[1536,512]{0,1:T(8,128)(2,1)} %convolution_convert_fusion.2, bf16[1536,1536]{0,1:T(8,128)(2,1)} %convolution_convert_fusion.1), dimensions={1} | concatenate | bytes 25171968 | tf_op jit(solution)/shard_map/concatenate | solution.py:75
  1041.6 16.6 copy.206
  1058.9 75.7 %all-gather.23.cloned.1.call-done = bf16[1024,6656]{1,0:T(8,128)(2,1)} async-done(((bf16[128,6656]{1,0:T(8,128)(2,1)}), bf16[1024,6656]{1,0:T(8,128)(2,1)}) %all-gather.23.cloned.1.call-update) | async-done | bytes 13631504 | tf_op jit(solution)/shard_map/all_gather | solution.py:23
  1142.5 11.9 copy.203
  1164.4 133.3 %reduce-scatter.9.cloned.1.call-done = bf16[192,4097]{1,0:T(8,128)(2,1)} async-done(((bf16[1536,4097]{1,0:T(8,128)(2,1)}), bf16[192,4097]{1,0:T(8,128)(2,1)}) %reduce-scatter.9.cloned.1.call-update) | async-done | bytes 1573264
  1304.7 279.1 %all-gather.21.cloned.1.call-done = bf16[1024,11784]{0,1:T(8,128)(2,1)} async-done(((bf16[128,11784]{0,1:T(8,128)(2,1)}), bf16[1024,11784]{0,1:T(8,128)(2,1)}) %all-gather.21.cloned.1.call-update) | async-done | bytes 24133648 | tf_op jit(solution)/shard_map/all_gather | solution.py:23
  1587.7 13.8 split.73
  1601.5 13.2 convolution_convert_fusion.5
  1635.4 56.9 %all-reduce.1 = (bf16[192]{0:T(256)(128)(2,1)S(1)}, bf16[192]{0:T(256)(128)(2,1)S(1)}, bf16[192,8]{0,1:T(8,128)(2,1)S(1)}) all-reduce(bf16[192]{0:T(256)(128)(2,1)S(1)} %slice_reduce_fusion, bf16[192]{0:T(256)(128)(2,1)S(1)} %reduce_sum.129, bf16[192,8]{0,1:T(8,128)(2,1)S(1)} %convolution_convert_fusion.6), channel_id=1, replica_groups=mesh['rep'=32,'fsdp'=8] {'rep'}, use_global_device_ids=true, to_apply=%region_14.15 | all-reduce | flops 1920 | bytes 7680 | tf_op jit(solution)/shard_map/psum | solution.py:335
  1694.1 177.8 %all-reduce.5.cloned.1.call-done = (bf16[192,1536]{0,1:T(8,128)(2,1)}, bf16[192,512]{0,1:T(8,128)(2,1)}, bf16[192,512]{0,1:T(8,128)(2,1)}, bf16[192,1536]{0,1:T(...) async-done(((bf16[192,1536]{0,1:T(8,128)(2,1)}, bf16[192,512]{0,1:T(8,128)(2,1)}, ...) | async-done | bytes 7471120 | tf_op jit(solution)/shard_map/psum | solution.py:336
  (260 shorter events, 192.4 us)
Async XLA Ops:
  7.2 120.2 %all-gather.11.cloned.1.call-start = ((), (), s32[]{:S(2)}) async-start(), calls=%async_computation.3 | async-start | bytes 9289728 | tf_op jit(solution)/shard_map/all_gather | solution.py:23
  10.7 187.1 %all-gather.13.cloned.1.call-start = ((), (), s32[]{:S(2)}) async-start(), calls=%async_computation.4 | async-start | bytes 2359296 | tf_op jit(solution)/shard_map/all_gather | solution.py:36
  10.9 182.5 %copy-start.48 = (f32[128]{0:T(128)}, f32[128]{0:T(128)S(1)}, u32[]{:S(2)}) copy-start(f32[128]{0:T(128)S(1)} %add_rsqrt_fusion.1) | copy-start | bytes 1540
  134.1 140.9 %all-gather.15.cloned.1.call-start = ((), (), s32[]{:S(2)}) async-start(), calls=%async_computation.5 | async-start | bytes 5308416 | tf_op jit(solution)/shard_map/all_gather | solution.py:173
  134.9 235.4 %all-gather.19.cloned.1.call-start = ((), (), s32[]{:S(2)}) async-start(), calls=%async_computation.7 | async-start | bytes 7077888 | tf_op jit(solution)/shard_map/all_gather | solution.py:178
  135.4 416.6 %all-gather.25.cloned.1.call-start = ((), (), s32[]{:S(2)}) async-start(), calls=%async_computation.10 | async-start | bytes 17694720 | tf_op jit(solution)/shard_map/all_gather | solution.py:47
  141.0 680.1 %all-gather.17.cloned.1.call-start = ((), (), s32[]{:S(2)}) async-start(), calls=%async_computation.6 | async-start | bytes 28311552 | tf_op jit(solution)/shard_map/all_gather | solution.py:179
  146.3 18.6 copy-start.52
  146.3 46.6 %copy-start.45 = (s32[1024]{0:T(1024)S(1)}, s32[1024]{0:T(1024)}, u32[]{:S(2)}) copy-start(s32[1024]{0:T(1024)} %param.16) | copy-start | bytes 12292
  146.3 46.7 %copy-start.53 = (s32[128,6]{0,1:T(8,128)S(1)}, s32[128,6]{0,1:T(8,128)}, u32[]{:S(2)}) copy-start(s32[128,6]{0,1:T(8,128)} %param.17) | copy-start | bytes 9220
  146.4 823.2 %reduce-scatter.7.cloned.1.call-start = ((), (), s32[]{:S(2)}) async-start(), calls=%async_computation.11 | async-start | bytes 2359296
  164.9 113.4 %copy-start.40 = (f32[1536]{0:T(1024)}, f32[1536]{0:T(1024)S(1)}, u32[]{:S(2)}) copy-start(f32[1536]{0:T(1024)S(1)} %convert_element_type.213) | copy-start | bytes 18436
  192.9 86.7 %copy-start.38 = (bf16[1536,8]{0,1:T(8,128)(2,1)}, bf16[1536,8]{0,1:T(8,128)(2,1)S(1)}, u32[]{:S(2)}) copy-start(bf16[1536,8]{0,1:T(8,128)(2,1)S(1)} %reshape.244) | copy-start | bytes 73732
  210.3 68.0 %copy-start.23 = (bf16[4,128,3,128]{3,1,2,0:T(8,128)(2,1)}, bf16[4,128,3,128]{3,1,2,0:T(8,128)(2,1)S(1)}, u32[]{:S(2)}) copy-start(bf16[4,128,3,128]{3,1,2,0:T(8,128)(2,1)S(1)} %fusion.45) | copy-start | bytes 1179652
  278.3 96.7 %copy-start.50 = (f32[128]{0:T(128)}, f32[128]{0:T(128)S(1)}, u32[]{:S(2)}) copy-start(f32[128]{0:T(128)S(1)} %add_rsqrt_fusion) | copy-start | bytes 1540
  279.3 95.7 %copy-start.8 = (bf16[128,1536]{1,0:T(8,128)(2,1)}, bf16[128,1536]{1,0:T(8,128)(2,1)S(1)}, u32[]{:S(2)}) copy-start(bf16[128,1536]{1,0:T(8,128)(2,1)S(1)} %multiply_convert_fusion.1) | copy-start | bytes 1179652
  586.6 13.2 copy-start.29
  599.8 221.3 %copy-start.9 = (bf16[128,1536]{1,0:T(8,128)(2,1)S(1)}, bf16[128,1536]{1,0:T(8,128)(2,1)}, u32[]{:S(2)}) copy-start(bf16[128,1536]{1,0:T(8,128)(2,1)} %copy-done.8) | copy-start | bytes 1179652
  601.7 229.4 %copy-start.30 = (bf16[128,1024]{1,0:T(8,128)(2,1)}, bf16[128,1024]{1,0:T(8,128)(2,1)S(1)}, u32[]{:S(2)}) copy-start(bf16[128,1024]{1,0:T(8,128)(2,1)S(1)} %get-tuple-element.106) | copy-start | bytes 786436
  892.0 242.6 %all-gather.23.cloned.1.call-start = ((), (), s32[]{:S(2)}) async-start(), calls=%async_computation.9 | async-start | bytes 15335424 | tf_op jit(solution)/shard_map/all_gather | solution.py:23
  901.5 396.1 %reduce-scatter.9.cloned.1.call-start = ((), (), s32[]{:S(2)}) async-start(), calls=%async_computation.12 | async-start | bytes 14598144
  1058.2 525.6 %all-gather.21.cloned.1.call-start = ((), (), s32[]{:S(2)}) async-start(), calls=%async_computation.8 | async-start | bytes 27150336 | tf_op jit(solution)/shard_map/all_gather | solution.py:23
  1058.8 813.1 %all-reduce.5.cloned.1.call-start = ((), (), s32[]{:S(2)}) async-start(), calls=%async_computation.13 | async-start | bytes 15990784 | tf_op jit(solution)/shard_map/psum | solution.py:336
  1620.8 11.4 all-to-all-start
  (51 other events, 269.6 us)
Sparse Core Ops, SparseCore 0:
  11.2 116.1 all-gather.10
  134.2 57.2 all-gather.12
  194.2 80.7 all-gather.14
  277.5 92.6 all-gather.18
  372.7 179.3 all-gather.24
  555.0 265.9 all-gather.16
  892.1 77.3 reduce-scatter.6
  972.5 162.0 all-gather.22
  1139.4 158.1 reduce-scatter.8
  1300.0 283.7 all-gather.20
  1619.6 252.2 all-reduce.4
where the time goes:
time: 1910 us; the launch traced here: 1900 us
  waiting for transfers between devices  1390 us (73%)
  local copies, waits for them, and re-layouts  231 us (12%)
  matrix products  130 us (7%)
  blocking collectives  101 us (5%)
  other arithmetic  23.5 us (1%)
    all_gather x3, waiting for transfers between devices, side_by_side(): whole = lax.all_gather(both, axis, axis=dim, tiled=True)  471 us
    all_gather x1, waiting for transfers between devices, shards(): lax.all_gather(w_expert_in, 'fsdp', axis=0, tiled=True)  219 us
    unnamed x13, waiting for transfers between devices  191 us
    psum x1, waiting for transfers between devices, shards(): lax.psum(attn_owned[1].astype(jnp.bfloat16), 'rep').astype(jnp.float32)  178 us
    all_gather x1, waiting for transfers between devices, gather_packed(): lines, at, gathered = (lax.all_gather(flat, axis), 0, [])  177 us
    all_gather x1, waiting for transfers between devices, shards(): lax.all_gather(w_shared_in, 'fsdp', axis=0, tiled=True)  88.5 us
    all_gather x1, waiting for transfers between devices, shards(): out_full = lax.all_gather(w_out, 'fsdp', axis=0, tiled=True)  64.7 us
    concatenate x1, local copies, waits for them, and re-layouts, sent_together(): both = jnp.concatenate(columns, axis=along)  63.8 us
  transfers between devices with their start and end apart: 12, of which 10 were waited for; matrix products, arithmetic and copies ran while one was open for 13% of the time, Pallas kernels for 0%

commit v1 on v0

v1 whole, which is shorter than its diff:
```python
import math

import jax
import jax.numpy as jnp
from jax import lax
from jax.sharding import Mesh, PartitionSpec as P

HEADS = 12
KV_HEADS = 4
HEAD = 128
GROUP = HEADS // KV_HEADS
D = 1536
FE = 512
FS = 1024
EXPERTS = 8
EPS = 1e-05
SCALE = 1.0 / math.sqrt(HEAD)

AXES = ("z", "ylo", "core", "yhi", "x")
SIZES = (8, 2, 2, 2, 4)
REP = ("z", "ylo", "core")
FSDP = ("yhi", "x")
PLANE = ("ylo", "yhi", "x")
BF = jnp.bfloat16
F32 = jnp.float32


def dot(left, right):
    return jnp.dot(left, right, preferred_element_type=F32)


def dot_rows(left, right):
    return lax.dot_general(left, right, (((1,), (1,)), ((), ())), preferred_element_type=F32)


def dot_cols(left, right):
    return lax.dot_general(left, right, (((0,), (0,)), ((), ())), preferred_element_type=F32)


def exchange(blocks, axes):
    return lax.all_to_all(blocks, axes, 0, 0, tiled=True)


def spread_x(rows):
    got = exchange(jnp.broadcast_to(rows[None], (4, *rows.shape)), "x")
    return got.reshape(4 * rows.shape[0], *rows.shape[1:])


def collect_x(rows):
    got = exchange(rows.reshape(4, rows.shape[0] // 4, *rows.shape[1:]), "x")
    return jnp.sum(got.astype(F32), axis=0)


def swap_core(rows):
    return lax.ppermute(rows, "core", [(0, 1), (1, 0)])


def pair_of_float(values):
    high = values.astype(BF)
    return high, (values - high.astype(F32)).astype(BF)


def normalize(values):
    factor = lax.rsqrt(jnp.mean(values * values, axis=-1, keepdims=True) + EPS)
    return values * factor, factor


def norm_back(grad_normed, unit, factor, gain):
    scaled = grad_normed * gain
    inner = jnp.mean(scaled * unit, axis=-1, keepdims=True)
    return factor * (scaled - unit * inner)


def silu_slope(values, sig):
    return sig * (1.0 + values * (1.0 - sig))


def shards(
    tokens,
    segment_ids,
    routes,
    gain_attn,
    w_query,
    w_key,
    w_value,
    w_out,
    gain_ffn,
    w_router,
    w_shared_in,
    w_shared_out,
    w_expert_in,
    w_expert_out,
    cotangent,
):
    core, half, place = (lax.axis_index(a) for a in ("core", "yhi", "x"))
    rows = tokens.shape[0]
    own = w_query.shape[0]

    slots = jnp.concatenate(
        [
            w_query.reshape(own, 4, GROUP * HEAD),
            w_key.reshape(own, 4, HEAD),
            w_value.reshape(own, 4, HEAD),
        ],
        axis=2,
    ).transpose(1, 0, 2)
    small = jnp.concatenate([gain_attn, gain_ffn, w_router.T.reshape(-1)]).reshape(3, 640)
    small = jnp.pad(small, ((0, 13), (0, 0)))
    slots = jnp.concatenate([slots, jnp.broadcast_to(small[None], (4, 16, 640))], axis=1)
    got = exchange(jnp.concatenate([slots, slots], axis=0), FSDP)
    w_qkv = got[:, :own].reshape(D, 640)
    small = got[:, own : own + 3].reshape(8, 1920)
    gain_one = small[:, :192].reshape(1, D).astype(F32)
    gain_two = small[:, 192:384].reshape(1, D).astype(F32)
    router = small[:, 384:].reshape(8, EXPERTS, 192).transpose(1, 0, 2).reshape(EXPERTS, D)

    all_tokens = spread_x(tokens)

    out_a = lax.ppermute(w_out, FSDP, [(b, (b % 2) * 4 + b // 2) for b in range(8)])
    out_b = lax.ppermute(w_out, FSDP, [(b, (1 - b % 2) * 4 + b // 2) for b in range(8)])
    w_o = jnp.concatenate(
        [jnp.where(half == 0, out_a, out_b), jnp.where(half == 0, out_b, out_a)], axis=0
    )

    of_core = lax.dynamic_index_in_dim(w_expert_in.reshape(own, 2, 4, 2 * FE), core, 1, False)
    of_shared = lax.dynamic_index_in_dim(w_shared_in.reshape(own, 2, 2, 4, 128), core, 2, False)
    of_shared = of_shared.transpose(2, 0, 1, 3).reshape(4, own, 256)
    slots = jnp.concatenate([of_core.transpose(1, 0, 2), of_shared], axis=2)
    w_in = exchange(jnp.concatenate([slots, slots], axis=0), FSDP).reshape(D, 1280)
    slots = lax.dynamic_index_in_dim(w_expert_out.reshape(2, 4, 64, D), core, 0, False)
    w_down = exchange(jnp.concatenate([slots, slots], axis=0), FSDP).reshape(FE, D)
    other = lax.ppermute(w_shared_out, ("core", "yhi"), [(0, 1), (3, 2)])
    w_down = jnp.concatenate([w_down, jnp.where(core == half, w_shared_out, other)], axis=0)

    grad_own = spread_x(cotangent)
    grad_all = jnp.concatenate([grad_own, swap_core(grad_own)], axis=0)

    inputs = tokens.astype(F32)
    unit_one, factor_one = normalize(all_tokens.astype(F32))
    normed_one = (unit_one * gain_one).astype(BF)
    qkv = dot(normed_one, w_qkv).astype(BF)
    kv_own = qkv[:, GROUP * HEAD :]
    kv_other = lax.ppermute(kv_own, "yhi", [(0, 1)])
    kv = jnp.concatenate([kv_own, kv_other], axis=0)
    keys, values = kv[:, :HEAD], kv[:, HEAD:]
    queries = qkv[:, : GROUP * HEAD].reshape(512, GROUP, HEAD).transpose(1, 0, 2)
    seg_own = lax.dynamic_slice_in_dim(segment_ids, half * 512, 512)
    seg_other = segment_ids[:512]
    pos = jnp.arange(512, dtype=jnp.int32)
    allowed_own = (pos[:, None] == pos[None, :]) | (pos[None, :] < pos[:, None]) & (
        seg_own[:, None] == seg_own[None, :]
    ) & (seg_own[None, :] != 0)
    allowed_other = (
        (seg_own[:, None] == seg_other[None, :]) & (seg_other[None, :] != 0) & (half == 1)
    )
    allowed = jnp.concatenate([allowed_own, allowed_other], axis=1)

    def scores_of():
        raw = jnp.einsum("gtd,sd->gts", queries, keys, preferred_element_type=F32) * SCALE
        return jnp.where(allowed[None], raw, -1e30)

    scores = scores_of()
    top_score = jnp.max(scores, axis=-1, keepdims=True)
    expo = jnp.exp(scores - top_score)
    total = jnp.sum(expo, axis=-1, keepdims=True)
    log_total = top_score + jnp.log(total)
    probs = (expo / total).astype(BF)
    attended = jnp.einsum("gts,sd->tgd", probs, values, preferred_element_type=F32)
    attended = attended.reshape(512, GROUP * HEAD).astype(BF)
    hidden = inputs + collect_x(dot(attended, w_o).astype(BF))

    unit_two, factor_two = normalize(hidden)
    normed_two = (unit_two * gain_two).astype(BF)
    logits = dot_rows(normed_two, router)
    chosen = jnp.sum(
        (routes[:, :, None] == jnp.arange(EXPERTS, dtype=jnp.int32)[None, None, :]).astype(F32),
        axis=1,
    )
    weighted = chosen * jnp.exp(logits)
    gates = weighted / jnp.sum(weighted, axis=-1, keepdims=True)
    packed = jnp.concatenate(
        [normed_two, *pair_of_float(gates), jnp.zeros((rows, 112), BF)], axis=1
    )
    packed = spread_x(packed)
    packed = jnp.concatenate([packed, swap_core(packed)], axis=0)
    normed_all = packed[:, :D]
    expert = core * 4 + place
    mine = (jnp.arange(EXPERTS, dtype=jnp.int32) == expert).astype(F32)[None]
    gates_all = packed[:, D : D + 8].astype(F32) + packed[:, D + 8 : D + 16].astype(F32)
    gate = jnp.sum(gates_all * mine, axis=1, keepdims=True)

    pre = dot(normed_all, w_in)
    gate_part, up_part = pre[:, :FE], pre[:, FE : 2 * FE]
    shared_gate, shared_up = pre[:, 2 * FE : 2 * FE + 128], pre[:, 2 * FE + 128 :]
    gate_sig = jax.nn.sigmoid(gate_part)
    activ = gate_part * gate_sig * up_part
    shared_sig = jax.nn.sigmoid(shared_gate)
    mixed = jnp.concatenate(
        [(gate * activ).astype(BF), (shared_gate * shared_sig * shared_up).astype(BF)], axis=1
    )
    back = dot_rows(grad_all, w_down)
    grad_mixed, grad_shared = back[:, :FE], back[:, FE:]
    grad_gate = jnp.sum(grad_mixed * activ, axis=1, keepdims=True)
    grad_activ = grad_mixed * gate
    grad_pre = jnp.concatenate(
        [
            (grad_activ * up_part * silu_slope(gate_part, gate_sig)).astype(BF),
            (grad_activ * gate_part * gate_sig).astype(BF),
            (grad_shared * shared_up * silu_slope(shared_gate, shared_sig)).astype(BF),
            (grad_shared * shared_gate * shared_sig).astype(BF),
        ],
        axis=1,
    )
    back_part = dot_rows(grad_pre, w_in).astype(BF)
    back_part = jnp.concatenate(
        [back_part, *pair_of_float(grad_gate * mine), jnp.zeros((1024, 112), BF)], axis=1
    )
    back_part = back_part[:512].astype(F32) + swap_core(back_part[512:]).astype(F32)
    back_sum = collect_x(back_part.astype(BF))

    result_part = dot(mixed, w_down).astype(BF)
    result_part = result_part[:512].astype(F32) + swap_core(result_part[512:]).astype(F32)
    result = (hidden + collect_x(result_part.astype(BF))).astype(BF)

    grad_in = dot_cols(normed_all, grad_pre).astype(BF)
    grad_down = dot_cols(mixed, grad_all).astype(BF)

    main = jnp.concatenate(
        [
            grad_in.reshape(8, 192, 10, 128).transpose(0, 2, 1, 3).reshape(8, 1920, 128),
            grad_down[:FE].reshape(8, 64, 12, 128).transpose(0, 2, 1, 3).reshape(8, 768, 128),
        ],
        axis=1,
    )
    main = main.reshape(8, 8, 2, 168, 128).transpose(1, 2, 0, 3, 4).reshape(8, 2, 1344, 128)
    side = grad_down[FE:].reshape(128, 12, 128).transpose(1, 0, 2).reshape(8, 2, 96, 128)
    flat = jnp.concatenate([main, side], axis=2)
    flat = lax.psum_scatter(flat, "z", scatter_dimension=0, tiled=True)[0]
    main = exchange(flat[:, :1344].reshape(16, 168, 128), PLANE).reshape(4, 4, 168, 128)
    main = jnp.sum(main.astype(F32), axis=0).astype(BF).reshape(672, 128)
    to = (jnp.arange(2) == core)[None, :, None, None]
    side = jnp.where(to, flat[:, None, 1344:], 0).reshape(4, 96, 128)
    side = jnp.sum(exchange(side, ("ylo", "yhi")).astype(F32), axis=0).astype(BF)
    whole = lax.all_gather(jnp.concatenate([main, side], axis=0), REP)
    main = whole[:, :672].reshape(16, 2, 4, 168, 128).transpose(1, 2, 0, 3, 4)
    main = main.reshape(8, 2688, 128)
    up = main[:, :1920].reshape(8, 10, 192, 128)
    sum_expert_in = up[:, :8].transpose(2, 0, 1, 3).reshape(192, 8, 1024).astype(F32)
    sum_shared_in = up[:, 8:].transpose(2, 1, 0, 3).reshape(192, 2048).astype(F32)
    sum_expert_out = main[:, 1920:].reshape(8, 12, 64, 128).transpose(0, 2, 1, 3)
    sum_expert_out = sum_expert_out.reshape(8, 64, D).astype(F32)
    side = whole[:, 672:].reshape(16, 2, 96, 128)
    side = lax.dynamic_index_in_dim(side, half, 1, False).reshape(12, 128, 128)
    sum_shared_out = side.transpose(1, 0, 2).reshape(128, D).astype(F32)

    grad_gates = back_sum[:, D : D + 8] + back_sum[:, D + 8 : D + 16]
    grad_logits = (
        gates * (grad_gates - jnp.sum(gates * grad_gates, axis=-1, keepdims=True))
    ).astype(BF)
    grad_normed_two = back_sum[:, :D] + dot(grad_logits, router)
    grad_router = dot_cols(grad_logits, normed_two)
    grad_gain_ffn = jnp.sum(grad_normed_two * unit_two, axis=0, keepdims=True)
    grad_hidden = cotangent.astype(F32) + norm_back(
        grad_normed_two, unit_two, factor_two, gain_two
    )
    hidden_low = spread_x(grad_hidden.astype(BF))

    grad_out = dot_cols(attended, hidden_low).astype(BF)
    grad_att = dot_rows(hidden_low, w_o).astype(BF)
    grad_heads = grad_att.reshape(512, GROUP, HEAD).transpose(1, 0, 2)
    probs_again = jnp.exp(scores_of() - log_total)
    grad_probs = jnp.einsum("gtd,sd->gts", grad_heads, values, preferred_element_type=F32)
    inner = jnp.sum(probs_again * grad_probs, axis=-1, keepdims=True)
    grad_scores = (probs_again * (grad_probs - inner)).astype(BF)
    grad_query = jnp.einsum("gts,sd->tgd", grad_scores, keys, preferred_element_type=F32) * SCALE
    grad_query = grad_query.reshape(512, GROUP * HEAD).astype(BF)
    grad_keys = jnp.einsum("gts,gtd->sd", grad_scores, queries, preferred_element_type=F32) * SCALE
    grad_values = jnp.einsum(
        "gts,gtd->sd", probs_again.astype(BF), grad_heads, preferred_element_type=F32
    )
    grad_kv = jnp.concatenate([grad_keys, grad_values], axis=1)
    from_other = lax.ppermute(grad_kv[512:].astype(BF), "yhi", [(1, 0)])
    grad_kv = (grad_kv[:512] + from_other.astype(F32)).astype(BF)
    grad_qkv = jnp.concatenate([grad_query, grad_kv], axis=1)
    grad_normed_one = dot_rows(grad_qkv, w_qkv)
    grad_gain_attn = jnp.sum(grad_normed_one * unit_one, axis=0, keepdims=True)
    grad_weights = dot_cols(normed_one, grad_qkv).astype(BF)

    small = jnp.concatenate([grad_router, grad_gain_ffn, grad_gain_attn], axis=0).astype(BF)
    small = small.reshape(10, 8, 192).transpose(1, 0, 2).reshape(8, 15, 128)
    small = jnp.pad(small, ((0, 0), (0, 49), (0, 0)))
    cols = grad_weights.reshape(8, 192, 5, 128).transpose(0, 2, 1, 3).reshape(8, 960, 128)
    cols = jnp.concatenate([cols, small], axis=1).reshape(8, 16, 2, 32, 128)
    cols = cols.transpose(2, 1, 0, 3, 4).reshape(2, 16, 256, 128)
    outs = grad_out.reshape(2, 192, 12, 128).transpose(0, 2, 1, 3).reshape(2, 16, 2, 72, 128)
    outs = outs.transpose(2, 1, 0, 3, 4).reshape(2, 16, 144, 128)
    flat = jnp.concatenate([cols, outs], axis=2)
    keep = lax.dynamic_index_in_dim(flat, core, 0, False)
    give = lax.dynamic_index_in_dim(flat, 1 - core, 0, False)
    flat = (keep.astype(F32) + swap_core(give).astype(F32)).astype(BF).reshape(8, 2, 400, 128)
    flat = lax.psum_scatter(flat, "z", scatter_dimension=0, tiled=True)[0]
    outs = lax.dynamic_update_slice(
        jnp.zeros((2, 8, 72, 128), BF), flat[:, 256:].reshape(2, 2, 72, 128), (0, 2 * place, 0, 0)
    )
    flat = jnp.concatenate([flat[:, :256].reshape(2, 8, 32, 128), outs], axis=2)
    got = exchange(flat.reshape(16, 104, 128), PLANE).reshape(4, 4, 104, 128)
    got = jnp.sum(got.astype(F32), axis=0)
    outs = jnp.sum(got[:, 32:], axis=0)
    whole = lax.all_gather(
        jnp.concatenate([got[:, :32].reshape(128, 128), outs], axis=0).astype(BF), REP
    )
    cols = whole[:, :128].reshape(32, 4, 32, 128).transpose(1, 0, 2, 3).reshape(4, 1024, 128)
    big = cols[:, :960].reshape(4, 5, 192, 128)
    sum_query = big[:, :3].transpose(2, 0, 1, 3).reshape(192, D).astype(F32)
    sum_key = big[:, 3].transpose(1, 0, 2).reshape(192, 512).astype(F32)
    sum_value = big[:, 4].transpose(1, 0, 2).reshape(192, 512).astype(F32)
    small = jnp.sum(cols[:, 960:975].astype(F32), axis=0).reshape(10, 192)
    sum_out = whole[:, 128:].reshape(12, 192, 128).transpose(1, 0, 2).reshape(192, D).astype(F32)

    back_one = collect_x(grad_normed_one.astype(BF))
    unit_own, factor_own = normalize(inputs)
    grad_input = (grad_hidden + norm_back(back_one, unit_own, factor_own, gain_one)).astype(BF)

    return (
        result,
        grad_input,
        small[9],
        sum_query,
        sum_key,
        sum_value,
        sum_out,
        small[8],
        small[:8].T,
        sum_shared_in,
        sum_shared_out,
        sum_expert_in,
        sum_expert_out,
    )


def solution(mesh):
    fine = Mesh(mesh.devices.reshape(SIZES), AXES)
    tokens = P((*REP, *FSDP), None)
    first = P(FSDP, None)
    return jax.shard_map(
        shards,
        mesh=fine,
        in_specs=(
            tokens,
            P(REP),
            tokens,
            P(FSDP),
            first,
            first,
            first,
            first,
            P(FSDP),
            first,
            first,
            first,
            P(FSDP, None, None),
            P(None, FSDP, None),
            tokens,
        ),
        out_specs=(
            tokens,
            tokens,
            P(FSDP),
            first,
            first,
            first,
            first,
            P(FSDP),
            first,
            first,
            first,
            P(FSDP, None, None),
            P(None, FSDP, None),
        ),
        check_vma=False,
    )
```

time: 1910 us -> 768 us (0.40)
  waiting for transfers between devices: 1390 us -> 361 us
  local copies, waits for them, and re-layouts: 231 us -> 125 us
  starting transfers between devices: 3.87 us -> 79.3 us
  matrix products: 130 us -> 62.1 us
  blocking collectives: 101 us -> 64.5 us
  other arithmetic: 23.5 us -> 48.9 us
    all_gather x8 -> x2, waiting for transfers between devices: 1020 us -> 81.3 us  [the longest x1 64.4 us: shards(): whole = lax.all_gather(jnp.concatenate([main, side], axis=0), REP)]
    unnamed x13 -> x4, waiting for transfers between devices: 191 us -> 0.07 us
    psum x1 -> x0, waiting for transfers between devices: 178 us -> none  [shards(): lax.psum(attn_owned[1].astype(jnp.bfloat16), 'rep').astype(jnp.float32)]
    all_to_all x1 -> x12, waiting for transfers between devices: 0.01 us -> 165 us  [exchange(): return lax.all_to_all(blocks, axes, 0, 0, tiled=True)]
    dot_general x19 -> x11, matrix products: 89.6 us -> 21.2 us  [the longest x5 13.2 us: dot(): return jnp.dot(left, right, preferred_element_type=F32)]
    all_to_all x0 -> x2, blocking collectives: none -> 64.5 us  [exchange(): return lax.all_to_all(blocks, axes, 0, 0, tiled=True)]
    ppermute x0 -> x10, waiting for transfers between devices: none -> 58.8 us  [the longest x1 41.1 us: shards(): other = lax.ppermute(w_shared_out, ('core', 'yhi'), [(0, 1), (3, 2)])]
    concatenate x2 -> x10, local copies, waits for them, and re-layouts: 66.4 us -> 8.57 us  [the longest x1 4.8 us: shards(): jnp.concatenate([back_part, *pair_of_float(grad_gate * mine), jnp.zeros((...]
  transfers between devices with their start and end apart: 12 -> 26, of which waited for: 10 -> 19; matrix products, arithmetic and copies ran while one was open for 13% -> 18% of each run, Pallas kernels for 0% -> 0%
where the time goes in v1:
time: 768 us; the launch traced here: 756 us
  waiting for transfers between devices  361 us (47%)
  local copies, waits for them, and re-layouts  125 us (16%)
  starting transfers between devices  79.3 us (10%)
  blocking collectives  64.5 us (8%)
  matrix products  62.1 us (8%)
  other arithmetic  48.9 us (6%)
  between operations  15.4 us (2%)
    all_to_all x12, waiting for transfers between devices, exchange(): return lax.all_to_all(blocks, axes, 0, 0, tiled=True)  165 us
    all_to_all x2, blocking collectives, exchange(): return lax.all_to_all(blocks, axes, 0, 0, tiled=True)  64.5 us
    all_gather x1, waiting for transfers between devices, shards(): whole = lax.all_gather(jnp.concatenate([main, side], axis=0), REP)  64.4 us
    reduce_scatter x2, waiting for transfers between devices, shards(): flat = lax.psum_scatter(flat, 'z', scatter_dimension=0, tiled=True)[0]  55.4 us
    all_to_all x12, starting transfers between devices, exchange(): return lax.all_to_all(blocks, axes, 0, 0, tiled=True)  52.4 us
    ppermute x1, waiting for transfers between devices, shards(): other = lax.ppermute(w_shared_out, ('core', 'yhi'), [(0, 1), (3, 2)])  41.1 us
    dot_general x5, matrix products, dot_rows(): lax.dot_general(left, right, (((1,), (1,)), ((), ())), preferred_element_...  20.5 us
    dot_general x5, matrix products, dot_cols(): lax.dot_general(left, right, (((0,), (0,)), ((), ())), preferred_element_...  20.4 us
  transfers between devices with their start and end apart: 26, of which 19 were waited for; matrix products, arithmetic and copies ran while one was open for 18% of the time, Pallas kernels for 0%

profile of v1, /device:TPU:1, one launch (start us, length us, event | category | flops | bytes accessed | tf_op | source)
XLA Modules:
  0.0 755.9 jit_solution(9600700596548906642)
XLA Ops:
  22.2 11.1 %all-to-all-done = bf16[4,128,1536]{2,1,0:T(8,128)(2,1)S(1)} async-done(((bf16[4,128,1536]{2,1,0:T(8,128)(2,1)}), bf16[4,128,1536]{2,1,0:T(8,128)(2,1)S(1)}, u32[]{:S(2)}, u32[]{:S(2)}) %all-to-all-start) | async-done | bytes 1572896 | tf_op jit(solution)/shard_map/all_to_all | solution.py:41
  48.5 19.6 %all-to-all-done.1 = bf16[8,208,640]{2,1,0:T(8,128)(2,1)} async-done(((bf16[8,208,640]{2,1,0:T(8,128)(2,1)}), bf16[8,208,640]{2,1,0:T(8,128)(2,1)}, u32[]{:S(2)}, u32[]{:S(2)}) %all-to-all-start.1) | async-done | bytes 2129952 | tf_op jit(solution)/shard_map/all_to_all | solution.py:41
  76.9 11.9 %collective-permute-done.2 = bf16[192,1536]{1,0:T(8,128)(2,1)} collective-permute-done((bf16[192,1536]{1,0:T(8,128)(2,1)}, bf16[192,1536]{1,0:T(8,128)(2,1)}, u32[]{:S(2)}, u32[]{:S(2)}) %collective-permute-start.2) | collective-permute-done | bytes 589856 | tf_op jit(solution)/shard_map/ppermute | solution.py:120
  99.8 50.9 %all_to_all.70 = bf16[4,128,1536]{2,1,0:T(8,128)(2,1)S(1)} all-to-all(bf16[4,128,1536]{2,1,0:T(8,128)(2,1)S(1)} %bitcast.283), channel_id=1, replica_groups=mesh['z'=8,'ylo'=2,'core'=2,'yhi'=2,'x'=4] {'x'}, dimensions={0} | all-to-all | bytes 3145728 | tf_op jit(solution)/shard_map/all_to_all | solution.py:41
  158.2 17.0 %all-to-all-done.7 = bf16[4,128,1536]{2,1,0:T(8,128)(2,1)} async-done(((bf16[4,128,1536]{2,1,0:T(8,128)(2,1)}), bf16[4,128,1536]{2,1,0:T(8,128)(2,1)}, u32[]{:S(2)}, u32[]{:S(2)}) %all-to-all-start.7) | async-done | bytes 1572896 | tf_op jit(solution)/shard_map/all_to_all | solution.py:41
  181.0 20.7 %all-to-all-done.5 = bf16[8,64,1536]{2,1,0:T(8,128)(2,1)S(1)} async-done(((bf16[8,64,1536]{2,1,0:T(8,128)(2,1)}), bf16[8,64,1536]{2,1,0:T(8,128)(2,1)S(1)}, u32[]{:S(2)}, u32[]{:S(2)}) %all-to-all-start.5) | async-done | bytes 1572896 | tf_op jit(solution)/shard_map/all_to_all | solution.py:41
  215.4 12.9 %all-to-all-done.3 = bf16[4,128,1664]{1,2,0:T(8,128)(2,1)S(1)} async-done(((bf16[4,128,1664]{1,2,0:T(8,128)(2,1)}), bf16[4,128,1664]{1,2,0:T(8,128)(2,1)S(1)}, u32[]{:S(2)}, u32[]{:S(2)}) %all-to-all-start.3) | async-done | bytes 1703968 | tf_op jit(solution)/shard_map/all_to_all | solution.py:41
  242.2 41.1 %collective-permute-done.4 = bf16[128,1536]{1,0:T(8,128)(2,1)} collective-permute-done((bf16[128,1536]{1,0:T(8,128)(2,1)}, bf16[128,1536]{1,0:T(8,128)(2,1)}, u32[]{:S(2)}, u32[]{:S(2)}) %collective-permute-start.4) | collective-permute-done | bytes 393248 | tf_op jit(solution)/shard_map/ppermute | solution.py:132
  293.9 7.5 fusion.9
  312.2 7.7 %convolution_convert_fusion.2 = bf16[1024,1536]{1,0:T(8,128)(2,1)} fusion(bf16[1536,1280]{1,0:T(8,128)(2,1)} %bitcast.17, bf16[1024,128]{1,0:T(8,128)(2,1)S(1)} %get-tuple-element.131, bf16[1024,128]{1,0:T(8,128)(2,1)S(1)} %get-tuple-element.130, bf16[1024,512]{1,0:T(8,128)(2,1)S(1)} %get-tuple-element.128, bf16[1024,512]{1,0:T(8,128)(2,1)S(1)} %get-tuple-element.127), kind=kOutput, calls=%fused_computation.18 | convolution fusion | flops 4038590464 | bytes 9699328 | tf_op jit(solution)/shard_map/dot_general | solution.py:33
  338.6 17.3 %all-to-all-done.6 = bf16[4,128,1536]{2,1,0:T(8,128)(2,1)} async-done(((bf16[4,128,1536]{2,1,0:T(8,128)(2,1)}), bf16[4,128,1536]{2,1,0:T(8,128)(2,1)}, u32[]{:S(2)}, u32[]{:S(2)}) %all-to-all-start.6) | async-done | bytes 1572896 | tf_op jit(solution)/shard_map/all_to_all | solution.py:41
  362.1 18.1 %all-to-all-done.8 = bf16[4,128,1664]{2,1,0:T(8,128)(2,1)S(1)} async-done(((bf16[4,128,1664]{2,1,0:T(8,128)(2,1)}), bf16[4,128,1664]{2,1,0:T(8,128)(2,1)S(1)}, u32[]{:S(2)}, u32[]{:S(2)}) %all-to-all-start.8) | async-done | bytes 1703968 | tf_op jit(solution)/shard_map/all_to_all | solution.py:41
  390.2 18.1 %all-to-all-done.9 = bf16[4,128,1536]{2,1,0:T(8,128)(2,1)} async-done(((bf16[4,128,1536]{2,1,0:T(8,128)(2,1)}), bf16[4,128,1536]{2,1,0:T(8,128)(2,1)}, u32[]{:S(2)}, u32[]{:S(2)}) %all-to-all-start.9) | async-done | bytes 1572896 | tf_op jit(solution)/shard_map/all_to_all | solution.py:41
  469.0 8.8 %convolution_convert_fusion = bf16[1536,1280]{1,0:T(8,128)(2,1)} fusion(bf16[1024,1664]{0,1:T(8,128)(2,1)} %constant_dynamic-update-slice_fusion, bf16[1024,128]{1,0:T(8,128)(2,1)S(1)} %copy-done.45, bf16[1024,128]{1,0:T(8,128)(2,1)S(1)} %copy-done.43, bf16[1024,512]{1,0:T(8,128)(2,1)S(1)} %copy-done.34, bf16[1024,512]{1,0:T(8,128)(2,1)S(1)} %copy-done.32), kind=kOutput, calls=%fused_computation | convolution fusion | flops 4038983680 | bytes 9699328 | tf_op jit(solution)/shard_map/dot_general | solution.py:37
  484.1 9.0 %reshape.436 = bf16[8,192,10,128]{1,0,3,2:T(8,128)(2,1)} reshape(bf16[1536,1280]{0,1:T(8,128)(2,1)} %copy.331) | data formatting | bytes 7864320 | tf_op jit(solution)/shard_map/reshape | solution.py:230
  493.1 8.4 %copy.332 = bf16[8,10,192,128]{3,2,1,0:T(8,128)(2,1)} copy(bf16[8,10,192,128]{2,0,3,1:T(8,128)(2,1)} %bitcast.239) | data formatting | bytes 7864320 | tf_op jit(solution)/shard_map/transpose | solution.py:230
  509.8 13.6 %all_to_all.71 = bf16[16,104,128]{2,1,0:T(8,128)(2,1)S(1)} all-to-all(bf16[16,104,128]{2,1,0:T(8,128)(2,1)S(1)} %pad_maximum_fusion.20), channel_id=1, replica_groups=mesh['z'=8,'ylo'=2,'core'=2,'yhi'=2,'x'=4] {'ylo','yhi','x'}, dimensions={0} | all-to-all | bytes 851968 | tf_op jit(solution)/shard_map/all_to_all | solution.py:41
  524.2 55.4 %reduce-scatter.5.cloned.1.call-done = bf16[1,2,1440,128]{3,2,1,0:T(8,128)(2,1)} async-done(((bf16[8,2,1440,128]{3,2,1,0:T(8,128)(2,1)}), bf16[1,2,1440,128]{3,2,1,0:T(8,128)(2,1)}) %reduce-scatter.5.cloned.1.call-update) | async-done | bytes 737296 | tf_op jit(solution)/shard_map/reduce_scatter | solution.py:238
  594.7 11.1 %all-to-all-done.12 = bf16[16,168,128]{2,1,0:T(8,128)(2,1)S(1)} async-done(((bf16[16,168,128]{2,1,0:T(8,128)(2,1)}), bf16[16,168,128]{2,1,0:T(8,128)(2,1)S(1)}, u32[]{:S(2)}, u32[]{:S(2)}) %all-to-all-start.12) | async-done | bytes 688160 | tf_op jit(solution)/shard_map/all_to_all | solution.py:41
  610.7 17.2 %all-to-all-done.10 = bf16[4,128,1536]{2,1,0:T(8,128)(2,1)S(1)} async-done(((bf16[4,128,1536]{2,1,0:T(8,128)(2,1)}), bf16[4,128,1536]{2,1,0:T(8,128)(2,1)S(1)}, u32[]{:S(2)}, u32[]{:S(2)}) %all-to-all-start.10) | async-done | bytes 1572896 | tf_op jit(solution)/shard_map/all_to_all | solution.py:41
  629.4 16.9 %all-gather.4.cloned.1.call-done = bf16[32,200,128]{2,1,0:T(8,128)(2,1)} async-done(((bf16[1,200,128]{2,1,0:T(8,128)(2,1)}), bf16[32,200,128]{2,1,0:T(8,128)(2,1)}) %all-gather.4.cloned.1.call-update) | async-done | bytes 1638416 | tf_op jit(solution)/shard_map/all_gather | solution.py:309
  653.6 64.4 %all-gather.6.cloned.1.call-done = bf16[24576,128]{1,0:T(8,128)(2,1)} async-done(((bf16[768,128]{1,0:T(8,128)(2,1)}), bf16[24576,128]{1,0:T(8,128)(2,1)}) %all-gather.6.cloned.1.call-update) | async-done | bytes 6291472 | tf_op jit(solution)/shard_map/all_gather | solution.py:244
  730.8 9.1 %copy.340 = f32[192,8,8,128]{3,2,1,0:T(8,128)} copy(f32[192,8,8,128]{3,0,2,1:T(8,128)} %convert_bitcast_fusion) | data formatting | bytes 12582912 | tf_op jit(solution)/shard_map/convert_element_type | solution.py:248
  739.9 7.2 reshape.462
  (343 shorter events, 265.6 us)
Async XLA Ops:
  9.6 23.7 %all-to-all-start = ((bf16[4,128,1536]{2,1,0:T(8,128)(2,1)}), bf16[4,128,1536]{2,1,0:T(8,128)(2,1)S(1)}, u32[]{:S(2)}, u32[]{:S(2)}) async-start(bf16[4,128,1536]{2,1,0:T(8,128)(2,1)} %broadcast_in_dim.51), calls=%async_computation | async-start | bytes 3145728 | tf_op jit(solution)/shard_map/all_to_all | solution.py:41
  33.3 34.8 %all-to-all-start.1 = ((bf16[8,208,640]{2,1,0:T(8,128)(2,1)}), bf16[8,208,640]{2,1,0:T(8,128)(2,1)}, u32[]{:S(2)}, u32[]{:S(2)}) async-start(bf16[8,208,640]{2,1,0:T(8,128)(2,1)} %copy.297), calls=%async_computation.1 | async-start | bytes 4259840 | tf_op jit(solution)/shard_map/all_to_all | solution.py:41
  39.1 37.8 %collective-permute-start.1 = (bf16[192,1536]{1,0:T(8,128)(2,1)}, bf16[192,1536]{1,0:T(8,128)(2,1)}, u32[]{:S(2)}, u32[]{:S(2)}) collective-permute-start(bf16[192,1536]{1,0:T(8,128)(2,1)} %param.22), channel_id=1, source_target_pairs={{0,0},{1,4},{2,1},{3,5},{4,2},{5,6},{6,3},{7,7},{8,8},{9,12},{10,9... | collective-permute-start | bytes 1769480 | tf_op jit(solution)/shard_map/ppermute | solution.py:119
  45.0 43.8 %collective-permute-start.2 = (bf16[192,1536]{1,0:T(8,128)(2,1)}, bf16[192,1536]{1,0:T(8,128)(2,1)}, u32[]{:S(2)}, u32[]{:S(2)}) collective-permute-start(bf16[192,1536]{1,0:T(8,128)(2,1)} %param.22), channel_id=1, source_target_pairs={{0,4},{1,0},{2,5},{3,1},{4,6},{5,2},{6,7},{7,3},{8,12},{9,8},{10,1... | collective-permute-start | bytes 1769480 | tf_op jit(solution)/shard_map/ppermute | solution.py:120
  72.7 20.3 %collective-permute-start = (bf16[512,256]{1,0:T(8,128)(2,1)S(1)}, bf16[512,256]{1,0:T(8,128)(2,1)S(1)}, u32[]{:S(2)}, u32[]{:S(2)}) collective-permute-start(bf16[512,256]{1,0:T(8,128)(2,1)S(1)} %slice.217), channel_id=1, source_target_pairs={{0,4},{1,5},{2,6},{3,7},{8,12},{9,13},{10,14},{11,15},{16,20},{17,... | collective-permute-start | bytes 786440 | tf_op jit(solution)/shard_map/ppermute | solution.py:143
  152.0 23.3 %all-to-all-start.7 = ((bf16[4,128,1536]{2,1,0:T(8,128)(2,1)}), bf16[4,128,1536]{2,1,0:T(8,128)(2,1)}, u32[]{:S(2)}, u32[]{:S(2)}) async-start(bf16[4,128,1536]{2,1,0:T(8,128)(2,1)} %broadcast_in_dim.64), calls=%async_computation.7 | async-start | bytes 3145728 | tf_op jit(solution)/shard_map/all_to_all | solution.py:41
  175.2 26.5 %all-to-all-start.5 = ((bf16[8,64,1536]{2,1,0:T(8,128)(2,1)}), bf16[8,64,1536]{2,1,0:T(8,128)(2,1)S(1)}, u32[]{:S(2)}, u32[]{:S(2)}) async-start(bf16[8,64,1536]{2,1,0:T(8,128)(2,1)} %pad_maximum_fusion.7), calls=%async_computation.5 | async-start | bytes 3145728 | tf_op jit(solution)/shard_map/all_to_all | solution.py:41
  203.4 24.9 %all-to-all-start.3 = ((bf16[4,128,1664]{1,2,0:T(8,128)(2,1)}), bf16[4,128,1664]{1,2,0:T(8,128)(2,1)S(1)}, u32[]{:S(2)}, u32[]{:S(2)}) async-start(bf16[4,128,1664]{1,2,0:T(8,128)(2,1)} %broadcast_in_dim.56), calls=%async_computation.3 | async-start | bytes 3407872 | tf_op jit(solution)/shard_map/all_to_all | solution.py:41
  228.3 65.6 %all-to-all-start.4 = ((bf16[8,192,1280]{2,1,0:T(8,128)(2,1)}), bf16[8,192,1280]{2,1,0:T(8,128)(2,1)}, u32[]{:S(2)}, u32[]{:S(2)}) async-start(bf16[8,192,1280]{2,1,0:T(8,128)(2,1)} %maximum_maximum_fusion), calls=%async_computation.4 | async-start | bytes 7864320 | tf_op jit(solution)/shard_map/all_to_all | solution.py:41
  232.8 51.5 %collective-permute-start.6 = (bf16[512,1536]{1,0:T(8,128)(2,1)}, bf16[512,1536]{1,0:T(8,128)(2,1)}, u32[]{:S(2)}, u32[]{:S(2)}) collective-permute-start(bf16[512,1536]{1,0:T(8,128)(2,1)} %bitcast.22), channel_id=1, source_target_pairs={{0,8},{8,0},{1,9},{9,1},{2,10},{10,2},{3,11},{11,3},{4,12},{12,4},... | collective-permute-start | bytes 4718600 | tf_op jit(solution)/shard_map/ppermute | solution.py:55
  234.7 48.6 %collective-permute-start.4 = (bf16[128,1536]{1,0:T(8,128)(2,1)}, bf16[128,1536]{1,0:T(8,128)(2,1)}, u32[]{:S(2)}, u32[]{:S(2)}) collective-permute-start(bf16[128,1536]{1,0:T(8,128)(2,1)} %param.26), channel_id=1, source_target_pairs={{0,4},{12,8},{1,5},{13,9},{2,6},{14,10},{3,7},{15,11},{16,20},{28,... | collective-permute-start | bytes 1179656 | tf_op jit(solution)/shard_map/ppermute | solution.py:132
  237.3 55.1 %collective-permute-start.3 = (bf16[512,1664]{0,1:T(8,128)(2,1)}, bf16[512,1664]{0,1:T(8,128)(2,1)S(1)}, u32[]{:S(2)}, u32[]{:S(2)}) collective-permute-start(bf16[512,1664]{0,1:T(8,128)(2,1)} %copy_bitcast_fusion.1), channel_id=1, source_target_pairs={{0,8},{8,0},{1,9},{9,1},{2,10},{10,2},{3,11},{11,3},{4,12},{12,4},... | collective-permute-start | bytes 5111816 | tf_op jit(solution)/shard_map/ppermute | solution.py:55
  310.4 16.9 %collective-permute-start.5 = (bf16[512,1536]{1,0:T(8,128)(2,1)}, bf16[512,1536]{1,0:T(8,128)(2,1)}, u32[]{:S(2)}, u32[]{:S(2)}) collective-permute-start(bf16[512,1536]{1,0:T(8,128)(2,1)} %slice.231), channel_id=1, source_target_pairs={{0,8},{8,0},{1,9},{9,1},{2,10},{10,2},{3,11},{11,3},{4,12},{12,4},... | collective-permute-start | bytes 4718600 | tf_op jit(solution)/shard_map/ppermute | solution.py:55
  326.8 8.7 %collective-permute-start.7 = (bf16[512,1664]{1,0:T(8,128)(2,1)}, bf16[512,1664]{1,0:T(8,128)(2,1)}, u32[]{:S(2)}, u32[]{:S(2)}) collective-permute-start(bf16[512,1664]{1,0:T(8,128)(2,1)} %slice.235), channel_id=1, source_target_pairs={{0,8},{8,0},{1,9},{9,1},{2,10},{10,2},{3,11},{11,3},{4,12},{12,4},... | collective-permute-start | bytes 5111816 | tf_op jit(solution)/shard_map/ppermute | solution.py:55
  330.9 25.0 %all-to-all-start.6 = ((bf16[4,128,1536]{2,1,0:T(8,128)(2,1)}), bf16[4,128,1536]{2,1,0:T(8,128)(2,1)}, u32[]{:S(2)}, u32[]{:S(2)}) async-start(bf16[4,128,1536]{2,1,0:T(8,128)(2,1)} %bitcast.258), calls=%async_computation.6 | async-start | bytes 3145728 | tf_op jit(solution)/shard_map/all_to_all | solution.py:41
  355.9 24.3 %all-to-all-start.8 = ((bf16[4,128,1664]{2,1,0:T(8,128)(2,1)}), bf16[4,128,1664]{2,1,0:T(8,128)(2,1)S(1)}, u32[]{:S(2)}, u32[]{:S(2)}) async-start(bf16[4,128,1664]{2,1,0:T(8,128)(2,1)} %bitcast.252), calls=%async_computation.8 | async-start | bytes 3407872 | tf_op jit(solution)/shard_map/all_to_all | solution.py:41
  385.2 23.0 %all-to-all-start.9 = ((bf16[4,128,1536]{2,1,0:T(8,128)(2,1)}), bf16[4,128,1536]{2,1,0:T(8,128)(2,1)}, u32[]{:S(2)}, u32[]{:S(2)}) async-start(bf16[4,128,1536]{2,1,0:T(8,128)(2,1)} %broadcast_in_dim.66), calls=%async_computation.9 | async-start | bytes 3145728 | tf_op jit(solution)/shard_map/all_to_all | solution.py:41
  389.7 118.1 %reduce-scatter.3.cloned.1.call-start = ((), (), s32[]{:S(2)}) async-start(), calls=%async_computation.16 | async-start | bytes 1843200 | tf_op jit(solution)/shard_map/reduce_scatter | solution.py:301
  420.3 8.7 %collective-permute-start.8 = (bf16[512,256]{0,1:T(8,128)(2,1)S(1)}, bf16[512,256]{0,1:T(8,128)(2,1)}, u32[]{:S(2)}, u32[]{:S(2)}) collective-permute-start(bf16[512,256]{0,1:T(8,128)(2,1)S(1)} %fusion.38), channel_id=1, source_target_pairs={{4,0},{5,1},{6,2},{7,3},{12,8},{13,9},{14,10},{15,11},{20,16},{21,... | collective-permute-start | bytes 786440 | tf_op jit(solution)/shard_map/ppermute | solution.py:282
  457.7 121.9 %reduce-scatter.5.cloned.1.call-start = ((), (), s32[]{:S(2)}) async-start(), calls=%async_computation.18 | async-start | bytes 6635520 | tf_op jit(solution)/shard_map/reduce_scatter | solution.py:238
  507.7 138.6 %all-gather.4.cloned.1.call-start = ((), (), s32[]{:S(2)}) async-start(), calls=%async_computation.17 | async-start | bytes 1689600 | tf_op jit(solution)/shard_map/all_gather | solution.py:309
  589.5 16.4 %all-to-all-start.12 = ((bf16[16,168,128]{2,1,0:T(8,128)(2,1)}), bf16[16,168,128]{2,1,0:T(8,128)(2,1)S(1)}, u32[]{:S(2)}, u32[]{:S(2)}) async-start(bf16[16,168,128]{2,1,0:T(8,128)(2,1)} %bitcast.84), calls=%async_computation.14 | async-start | bytes 1376256 | tf_op jit(solution)/shard_map/all_to_all | solution.py:41
  594.7 123.3 %all-gather.6.cloned.1.call-start = ((), (), s32[]{:S(2)}) async-start(), calls=%async_computation.19 | async-start | bytes 6488064 | tf_op jit(solution)/shard_map/all_gather | solution.py:244
  606.8 21.1 %all-to-all-start.10 = ((bf16[4,128,1536]{2,1,0:T(8,128)(2,1)}), bf16[4,128,1536]{2,1,0:T(8,128)(2,1)S(1)}, u32[]{:S(2)}, u32[]{:S(2)}) async-start(bf16[4,128,1536]{2,1,0:T(8,128)(2,1)} %bitcast.279), calls=%async_computation.10 | async-start | bytes 3145728 | tf_op jit(solution)/shard_map/all_to_all | solution.py:41
  (63 other events, 698.4 us)
Sparse Core Ops, SparseCore 0:
  457.8 36.8 reduce-scatter.2
  507.9 71.6 reduce-scatter.4
  582.2 64.1 all-gather.3
  648.8 69.1 all-gather.5

commit v2 on v1

--- a/solution.py
+++ b/solution.py
@@ -21,6 +21,7 @@
 REP = ("z", "ylo", "core")
 FSDP = ("yhi", "x")
 PLANE = ("ylo", "yhi", "x")
+KEY_HEAD = (0, 2, 1, 3)
 BF = jnp.bfloat16
 F32 = jnp.float32
 
@@ -41,14 +42,53 @@
     return lax.all_to_all(blocks, axes, 0, 0, tiled=True)
 
 
+def up_x(rows):
+    return lax.ppermute(rows, "x", [(i, (i + 1) % 4) for i in range(4)])
+
+
+def down_x(rows):
+    return lax.ppermute(rows, "x", [(i, (i + 3) % 4) for i in range(4)])
+
+
 def spread_x(rows):
-    got = exchange(jnp.broadcast_to(rows[None], (4, *rows.shape)), "x")
-    return got.reshape(4 * rows.shape[0], *rows.shape[1:])
+    cut = rows.shape[0] // 2
+    below, above = up_x(rows), down_x(rows)
+    far = up_x(below[:cut]), down_x(above[cut:])
+    return jnp.concatenate([rows, below, above, *far], axis=0)
 
 
 def collect_x(rows):
-    got = exchange(rows.reshape(4, rows.shape[0] // 4, *rows.shape[1:]), "x")
-    return jnp.sum(got.astype(F32), axis=0)
+    size = rows.shape[0] // 4
+    cut = size // 2
+    own, below, above, far = (rows[k * size : (k + 1) * size] for k in range(4))
+    far_up, far_down = up_x(far[:cut]), down_x(far[cut:])
+    above = jnp.concatenate([plus(above[:cut], far_up), above[cut:]], axis=0)
+    below = jnp.concatenate([below[:cut], plus(below[cut:], far_down)], axis=0)
+    return own.astype(F32) + up_x(above).astype(F32) + down_x(below).astype(F32)
+
+
+def plus(left, right):
+    return (left.astype(F32) + right.astype(F32)).astype(BF)
+
+
+def spread_z(rows, level):
+    up = [(i, (i + 1) % 8) for i in range(8)]
+    down = [(i, (i + 7) % 8) for i in range(8)]
+    cut = rows.shape[0] // 2
+    whole = jnp.zeros((8, *rows.shape), rows.dtype)
+
+    def put(whole, block, distance, start=0):
+        return lax.dynamic_update_slice(
+            whole, block[None], (lax.rem(level + distance + 8, 8), start, 0)
+        )
+
+    whole = put(whole, rows, 0)
+    below = above = rows
+    for k in (1, 2, 3):
+        below, above = lax.ppermute(below, "z", up), lax.ppermute(above, "z", down)
+        whole = put(put(whole, below, -k), above, k)
+    whole = put(whole, lax.ppermute(below[:cut], "z", up), 4)
+    return put(whole, lax.ppermute(above[cut:], "z", down), 4, cut)
 
 
 def swap_core(rows):
@@ -96,6 +136,11 @@
     rows = tokens.shape[0]
     own = w_query.shape[0]
 
+    level = lax.axis_index("z")
+    member = half * 4 + place
+    key_head = jnp.array(KEY_HEAD, jnp.int32)[place]
+
+    all_tokens = spread_x(tokens)
     slots = jnp.concatenate(
         [
             w_query.reshape(own, 4, GROUP * HEAD),
@@ -103,32 +148,56 @@
             w_value.reshape(own, 4, HEAD),
         ],
         axis=2,
-    ).transpose(1, 0, 2)
+    )
+    slots = lax.dynamic_slice_in_dim(slots, core * 96, 96, 0)
+    slots = jnp.stack([slots[:, k] for k in KEY_HEAD])
     small = jnp.concatenate([gain_attn, gain_ffn, w_router.T.reshape(-1)]).reshape(3, 640)
-    small = jnp.pad(small, ((0, 13), (0, 0)))
-    slots = jnp.concatenate([slots, jnp.broadcast_to(small[None], (4, 16, 640))], axis=1)
+    small = jnp.pad(small, ((0, 5), (0, 0)))
+    slots = jnp.concatenate([slots, jnp.broadcast_to(small[None], (4, 8, 640))], axis=1)
     got = exchange(jnp.concatenate([slots, slots], axis=0), FSDP)
-    w_qkv = got[:, :own].reshape(D, 640)
-    small = got[:, own : own + 3].reshape(8, 1920)
+    mine, other = got[:, :96], swap_core(got[:, :96])
+    w_qkv = jnp.stack(
+        [jnp.where(core == 0, mine, other), jnp.where(core == 0, other, mine)], axis=1
+    ).reshape(D, 640)
+    small = got[:, 96:99].reshape(8, 1920)
     gain_one = small[:, :192].reshape(1, D).astype(F32)
     gain_two = small[:, 192:384].reshape(1, D).astype(F32)
     router = small[:, 384:].reshape(8, EXPERTS, 192).transpose(1, 0, 2).reshape(EXPERTS, D)
 
-    all_tokens = spread_x(tokens)
-
-    out_a = lax.ppermute(w_out, FSDP, [(b, (b % 2) * 4 + b // 2) for b in range(8)])
-    out_b = lax.ppermute(w_out, FSDP, [(b, (1 - b % 2) * 4 + b // 2) for b in range(8)])
+    mine = lax.ppermute(
+        w_out,
+        ("core", "yhi", "x"),
+        [(s * 8 + b, (b % 2) * 8 + s * 4 + KEY_HEAD[b // 2]) for s in range(2) for b in range(8)],
+    )
+    other = swap_core(mine)
     w_o = jnp.concatenate(
-        [jnp.where(half == 0, out_a, out_b), jnp.where(half == 0, out_b, out_a)], axis=0
-    )
-
-    of_core = lax.dynamic_index_in_dim(w_expert_in.reshape(own, 2, 4, 2 * FE), core, 1, False)
-    of_shared = lax.dynamic_index_in_dim(w_shared_in.reshape(own, 2, 2, 4, 128), core, 2, False)
-    of_shared = of_shared.transpose(2, 0, 1, 3).reshape(4, own, 256)
-    slots = jnp.concatenate([of_core.transpose(1, 0, 2), of_shared], axis=2)
-    w_in = exchange(jnp.concatenate([slots, slots], axis=0), FSDP).reshape(D, 1280)
-    slots = lax.dynamic_index_in_dim(w_expert_out.reshape(2, 4, 64, D), core, 0, False)
-    w_down = exchange(jnp.concatenate([slots, slots], axis=0), FSDP).reshape(FE, D)
+        [jnp.where(core == 0, mine, other), jnp.where(core == 0, other, mine)], axis=0
+    )
+
+    target = core * 4 + (member - level + 8) % 4
+    block = jnp.concatenate(
+        [
+            lax.dynamic_index_in_dim(w_expert_in, target, 1, False),
+            lax.dynamic_slice_in_dim(w_shared_in, target * 128, 128, 1),
+            lax.dynamic_slice_in_dim(w_shared_in, FS + target * 128, 128, 1),
+            lax.dynamic_index_in_dim(w_expert_out, target, 0, False)
+            .reshape(64, 3, 512)
+            .transpose(1, 0, 2)
+            .reshape(192, 512),
+        ],
+        axis=1,
+    )
+    block = lax.ppermute(
+        block,
+        ("z", *FSDP),
+        [(z * 8 + b, z * 8 + (b - z) % 8) for z in range(8) for b in range(8)],
+    )
+    blocks = lax.all_gather(block, "z")
+    blocks = jnp.stack(
+        [lax.dynamic_index_in_dim(blocks, (b - member + 8) % 8, 0, False) for b in range(8)]
+    )
+    w_in = blocks[:, :, :1280].reshape(D, 1280)
+    w_down = blocks[:, :, 1280:].reshape(8, 3, 64, 512).transpose(0, 2, 1, 3).reshape(FE, D)
     other = lax.ppermute(w_shared_out, ("core", "yhi"), [(0, 1), (3, 2)])
     w_down = jnp.concatenate([w_down, jnp.where(core == half, w_shared_out, other)], axis=0)
 
@@ -144,9 +213,12 @@
     kv = jnp.concatenate([kv_own, kv_other], axis=0)
     keys, values = kv[:, :HEAD], kv[:, HEAD:]
     queries = qkv[:, : GROUP * HEAD].reshape(512, GROUP, HEAD).transpose(1, 0, 2)
-    seg_own = lax.dynamic_slice_in_dim(segment_ids, half * 512, 512)
-    seg_other = segment_ids[:512]
-    pos = jnp.arange(512, dtype=jnp.int32)
+    starts = [lax.rem(place + k, 4) * 128 for k in (0, 3, 1, 2)]
+    pos = jnp.concatenate([s + jnp.arange(128, dtype=jnp.int32) for s in starts])
+    seg_own = jnp.concatenate(
+        [lax.dynamic_slice_in_dim(segment_ids, half * 512 + s, 128) for s in starts]
+    )
+    seg_other = jnp.concatenate([lax.dynamic_slice_in_dim(segment_ids, s, 128) for s in starts])
     allowed_own = (pos[:, None] == pos[None, :]) | (pos[None, :] < pos[:, None]) & (
         seg_own[:, None] == seg_own[None, :]
     ) & (seg_own[None, :] != 0)
@@ -227,38 +299,45 @@
 
     main = jnp.concatenate(
         [
-            grad_in.reshape(8, 192, 10, 128).transpose(0, 2, 1, 3).reshape(8, 1920, 128),
-            grad_down[:FE].reshape(8, 64, 12, 128).transpose(0, 2, 1, 3).reshape(8, 768, 128),
+            grad_in.reshape(8, 8, 24, 1280),
+            grad_down[:FE]
+            .reshape(8, 64, 3, 512)
+            .transpose(0, 2, 1, 3)
+            .reshape(8, 8, 24, 512),
         ],
-        axis=1,
-    )
-    main = main.reshape(8, 8, 2, 168, 128).transpose(1, 2, 0, 3, 4).reshape(8, 2, 1344, 128)
-    side = grad_down[FE:].reshape(128, 12, 128).transpose(1, 0, 2).reshape(8, 2, 96, 128)
-    flat = jnp.concatenate([main, side], axis=2)
+        axis=3,
+    )
+    main = main.transpose(1, 0, 2, 3).reshape(8, 192, 1792)
+    side = jnp.pad(grad_down[FE:].reshape(8, 16, D), ((0, 0), (0, 0), (0, 256)))
+    flat = jnp.concatenate([main, side], axis=1)
     flat = lax.psum_scatter(flat, "z", scatter_dimension=0, tiled=True)[0]
-    main = exchange(flat[:, :1344].reshape(16, 168, 128), PLANE).reshape(4, 4, 168, 128)
-    main = jnp.sum(main.astype(F32), axis=0).astype(BF).reshape(672, 128)
+    main = flat[:192].reshape(8, 24, 2, 896).transpose(2, 0, 1, 3).reshape(16, 24, 896)
+    main = exchange(main, PLANE).reshape(4, 4, 24, 896)
+    main = jnp.sum(main.astype(F32), axis=0).astype(BF).reshape(96, 896)
     to = (jnp.arange(2) == core)[None, :, None, None]
-    side = jnp.where(to, flat[:, None, 1344:], 0).reshape(4, 96, 128)
+    side = flat[192:, :D].reshape(16, 2, 768).transpose(1, 0, 2)
+    side = jnp.where(to, side[:, None], 0).reshape(4, 16, 768)
     side = jnp.sum(exchange(side, ("ylo", "yhi")).astype(F32), axis=0).astype(BF)
+    side = jnp.pad(side, ((0, 0), (0, 128)))
     whole = lax.all_gather(jnp.concatenate([main, side], axis=0), REP)
-    main = whole[:, :672].reshape(16, 2, 4, 168, 128).transpose(1, 2, 0, 3, 4)
-    main = main.reshape(8, 2688, 128)
-    up = main[:, :1920].reshape(8, 10, 192, 128)
-    sum_expert_in = up[:, :8].transpose(2, 0, 1, 3).reshape(192, 8, 1024).astype(F32)
-    sum_shared_in = up[:, 8:].transpose(2, 1, 0, 3).reshape(192, 2048).astype(F32)
-    sum_expert_out = main[:, 1920:].reshape(8, 12, 64, 128).transpose(0, 2, 1, 3)
-    sum_expert_out = sum_expert_out.reshape(8, 64, D).astype(F32)
-    side = whole[:, 672:].reshape(16, 2, 96, 128)
-    side = lax.dynamic_index_in_dim(side, half, 1, False).reshape(12, 128, 128)
-    sum_shared_out = side.transpose(1, 0, 2).reshape(128, D).astype(F32)
+    whole = whole.reshape(8, 2, 2, 112, 896)
+    main = whole[:, :, :, :96].reshape(8, 2, 8, 24, 896)
+    low, high = main[:, 0], main[:, 1]
+    sum_expert_in = jnp.concatenate([low, high[..., :128]], axis=-1)
+    sum_expert_in = sum_expert_in.transpose(0, 2, 1, 3).reshape(192, 8, 1024).astype(F32)
+    sum_shared_in = high[..., 128:384].reshape(8, 8, 24, 2, 128).transpose(0, 2, 3, 1, 4)
+    sum_shared_in = sum_shared_in.reshape(192, 2048).astype(F32)
+    sum_expert_out = high[..., 384:].transpose(1, 0, 2, 3).reshape(8, 3, 64, 512)
+    sum_expert_out = sum_expert_out.transpose(0, 2, 1, 3).reshape(8, 64, D).astype(F32)
+    side = lax.dynamic_index_in_dim(whole[:, :, :, 96:, :768], half, 2, False)
+    sum_shared_out = side.transpose(0, 2, 1, 3).reshape(128, D).astype(F32)
 
     grad_gates = back_sum[:, D : D + 8] + back_sum[:, D + 8 : D + 16]
     grad_logits = (
         gates * (grad_gates - jnp.sum(gates * grad_gates, axis=-1, keepdims=True))
     ).astype(BF)
     grad_normed_two = back_sum[:, :D] + dot(grad_logits, router)
-    grad_router = dot_cols(grad_logits, normed_two)
+    grad_router = dot_cols(normed_two, jnp.pad(grad_logits, ((0, 0), (0, 120))))
     grad_gain_ffn = jnp.sum(grad_normed_two * unit_two, axis=0, keepdims=True)
     grad_hidden = cotangent.astype(F32) + norm_back(
         grad_normed_two, unit_two, factor_two, gain_two
@@ -286,36 +365,37 @@
     grad_gain_attn = jnp.sum(grad_normed_one * unit_one, axis=0, keepdims=True)
     grad_weights = dot_cols(normed_one, grad_qkv).astype(BF)
 
-    small = jnp.concatenate([grad_router, grad_gain_ffn, grad_gain_attn], axis=0).astype(BF)
-    small = small.reshape(10, 8, 192).transpose(1, 0, 2).reshape(8, 15, 128)
-    small = jnp.pad(small, ((0, 0), (0, 49), (0, 0)))
-    cols = grad_weights.reshape(8, 192, 5, 128).transpose(0, 2, 1, 3).reshape(8, 960, 128)
-    cols = jnp.concatenate([cols, small], axis=1).reshape(8, 16, 2, 32, 128)
-    cols = cols.transpose(2, 1, 0, 3, 4).reshape(2, 16, 256, 128)
-    outs = grad_out.reshape(2, 192, 12, 128).transpose(0, 2, 1, 3).reshape(2, 16, 2, 72, 128)
-    outs = outs.transpose(2, 1, 0, 3, 4).reshape(2, 16, 144, 128)
-    flat = jnp.concatenate([cols, outs], axis=2)
+    gains = jnp.concatenate([grad_gain_ffn, grad_gain_attn], axis=0).T
+    small = (grad_router + jnp.pad(gains, ((0, 0), (8, 118)))).astype(BF)
+    cols = jnp.concatenate([grad_weights, small], axis=1).reshape(8, 8, 24, 2, 384)
+    cols = cols.transpose(3, 1, 0, 2, 4).reshape(2, 8, 192, 384)
+    outs = grad_out.reshape(2, 8, 24, 2, 2, 384).transpose(3, 1, 0, 4, 2, 5)
+    flat = jnp.concatenate([cols, outs.reshape(2, 8, 96, 384)], axis=2)
     keep = lax.dynamic_index_in_dim(flat, core, 0, False)
     give = lax.dynamic_index_in_dim(flat, 1 - core, 0, False)
-    flat = (keep.astype(F32) + swap_core(give).astype(F32)).astype(BF).reshape(8, 2, 400, 128)
-    flat = lax.psum_scatter(flat, "z", scatter_dimension=0, tiled=True)[0]
+    flat = exchange(plus(keep, swap_core(give)), "z")
+    flat = jnp.sum(flat.astype(F32), axis=0).astype(BF)
     outs = lax.dynamic_update_slice(
-        jnp.zeros((2, 8, 72, 128), BF), flat[:, 256:].reshape(2, 2, 72, 128), (0, 2 * place, 0, 0)
-    )
-    flat = jnp.concatenate([flat[:, :256].reshape(2, 8, 32, 128), outs], axis=2)
-    got = exchange(flat.reshape(16, 104, 128), PLANE).reshape(4, 4, 104, 128)
+        jnp.zeros((8, 48, 384), BF), flat[192:].reshape(2, 48, 384), (2 * key_head, 0, 0)
+    )
+    flat = jnp.concatenate([flat[:192].reshape(8, 24, 384), outs], axis=1)
+    got = exchange(jnp.concatenate([flat, flat], axis=0), PLANE).reshape(4, 4, 72, 384)
     got = jnp.sum(got.astype(F32), axis=0)
-    outs = jnp.sum(got[:, 32:], axis=0)
-    whole = lax.all_gather(
-        jnp.concatenate([got[:, :32].reshape(128, 128), outs], axis=0).astype(BF), REP
-    )
-    cols = whole[:, :128].reshape(32, 4, 32, 128).transpose(1, 0, 2, 3).reshape(4, 1024, 128)
-    big = cols[:, :960].reshape(4, 5, 192, 128)
-    sum_query = big[:, :3].transpose(2, 0, 1, 3).reshape(192, D).astype(F32)
-    sum_key = big[:, 3].transpose(1, 0, 2).reshape(192, 512).astype(F32)
-    sum_value = big[:, 4].transpose(1, 0, 2).reshape(192, 512).astype(F32)
-    small = jnp.sum(cols[:, 960:975].astype(F32), axis=0).reshape(10, 192)
-    sum_out = whole[:, 128:].reshape(12, 192, 128).transpose(1, 0, 2).reshape(192, D).astype(F32)
+    outs = jnp.sum(got[:, 24:], axis=0)
+    mine = jnp.concatenate([got[:, :24].reshape(96, 384), outs], axis=0).astype(BF)
+    mine = spread_z(mine, level)
+    other = swap_core(mine)
+    first, second = jnp.where(core == 0, mine, other), jnp.where(core == 0, other, mine)
+    cols = first[:, :96].reshape(8, 4, 24, 384)
+    cols = jnp.stack([cols[:, k] for k in KEY_HEAD], axis=2)
+    sum_query = cols.reshape(192, D).astype(F32)
+    cols = second[:, :96].reshape(8, 4, 24, 3, 128)
+    small = jnp.sum(cols[..., 2, :].astype(F32), axis=1).reshape(192, 128)
+    cols = jnp.stack([cols[:, k] for k in KEY_HEAD], axis=2)
+    sum_key = cols[:, :, :, 0].reshape(192, 512).astype(F32)
+    sum_value = cols[:, :, :, 1].reshape(192, 512).astype(F32)
+    outs = jnp.stack([first[:, 96:], second[:, 96:]], axis=1).reshape(8, 4, 24, 384)
+    sum_out = outs.transpose(0, 2, 1, 3).reshape(192, D).astype(F32)
 
     back_one = collect_x(grad_normed_one.astype(BF))
     unit_own, factor_own = normalize(inputs)
@@ -324,13 +404,13 @@
     return (
         result,
         grad_input,
-        small[9],
+        small[:, 9],
         sum_query,
         sum_key,
         sum_value,
         sum_out,
-        small[8],
-        small[:8].T,
+        small[:, 8],
+        small[:, :8],
         sum_shared_in,
         sum_shared_out,
         sum_expert_in,

time: 768 us -> 573 us (0.75)
  waiting for transfers between devices: 361 us -> 141 us
  starting transfers between devices: 79.3 us -> 159 us
  blocking collectives: 64.5 us -> 0 us
  local copies, waits for them, and re-layouts: 125 us -> 138 us
  other arithmetic: 48.9 us -> 60.6 us
  matrix products: 62.1 us -> 50.9 us
    all_to_all x12 -> x5, waiting for transfers between devices: 165 us -> 58.6 us  [exchange(): return lax.all_to_all(blocks, axes, 0, 0, tiled=True)]
    ppermute x2 -> x42, starting transfers between devices: 7.64 us -> 80.8 us  [the longest x16 44.1 us: down_x(): return lax.ppermute(rows, 'x', [(i, (i + 3) % 4) for i in range(4)])]
    all_to_all x2 -> x0, blocking collectives: 64.5 us -> none  [exchange(): return lax.all_to_all(blocks, axes, 0, 0, tiled=True)]
    all_gather x1, waiting for transfers between devices: 64.4 us -> 0.01 us  [shards(): whole = lax.all_gather(jnp.concatenate([main, side], axis=0), REP)]
    ppermute x2 -> x42, waiting for transfers between devices: 11.9 us -> 67.9 us  [the longest x16 31.2 us: up_x(): return lax.ppermute(rows, 'x', [(i, (i + 1) % 4) for i in range(4)])]
    reduce_scatter x2 -> x1, waiting for transfers between devices: 55.4 us -> 0.01 us  [shards(): flat = lax.psum_scatter(flat, 'z', scatter_dimension=0, tiled=True)[0]]
    ppermute x1, waiting for transfers between devices: 41.1 us -> 8.72 us  [shards(): other = lax.ppermute(w_shared_out, ('core', 'yhi'), [(0, 1), (3, 2)])]
    unnamed x123 -> x188, local copies, waits for them, and re-layouts: 13.6 us -> 35.8 us
  transfers between devices with their start and end apart: 26 -> 61, of which waited for: 19 -> 26; matrix products, arithmetic and copies ran while one was open for 18% -> 30% of each run, Pallas kernels for 0% -> 0%
where the time goes in v2:
time: 573 us; the launch traced here: 566 us
  starting transfers between devices  159 us (28%)
  waiting for transfers between devices  141 us (25%)
  local copies, waits for them, and re-layouts  138 us (24%)
  other arithmetic  60.6 us (11%)
  matrix products  50.9 us (9%)
  between operations  16.8 us (3%)
    all_to_all x5, waiting for transfers between devices, exchange(): return lax.all_to_all(blocks, axes, 0, 0, tiled=True)  58.6 us
    ppermute x16, starting transfers between devices, down_x(): return lax.ppermute(rows, 'x', [(i, (i + 3) % 4) for i in range(4)])  44.1 us
    all_to_all x5, starting transfers between devices, exchange(): return lax.all_to_all(blocks, axes, 0, 0, tiled=True)  41.7 us
    unnamed x188, local copies, waits for them, and re-layouts  35.8 us
    ppermute x16, waiting for transfers between devices, up_x(): return lax.ppermute(rows, 'x', [(i, (i + 1) % 4) for i in range(4)])  31.2 us
    ppermute x8, starting transfers between devices, swap_core(): return lax.ppermute(rows, 'core', [(0, 1), (1, 0)])  29.1 us
    ppermute x16, waiting for transfers between devices, down_x(): return lax.ppermute(rows, 'x', [(i, (i + 3) % 4) for i in range(4)])  26.3 us
    dot_general x5, matrix products, dot_rows(): lax.dot_general(left, right, (((1,), (1,)), ((), ())), preferred_element_...  16.9 us
  transfers between devices with their start and end apart: 61, of which 26 were waited for; matrix products, arithmetic and copies ran while one was open for 30% of the time, Pallas kernels for 0%

profile of v2, /device:TPU:1, one launch (start us, length us, event | category | flops | bytes accessed | tf_op | source)
XLA Modules:
  0.0 566.2 jit_solution(12189730928902114902)
XLA Ops:
  20.3 5.5 all-to-all-start
  25.9 6.7 %collective-permute-start.6 = (bf16[192,1536]{1,0:T(8,128)(2,1)}, bf16[192,1536]{1,0:T(8,128)(2,1)}, u32[]{:S(2)}, u32[]{:S(2)}) collective-permute-start(bf16[192,1536]{1,0:T(8,128)(2,1)} %param.23), channel_id=1, source_target_pairs={{0,0},{1,8},{2,2},{3,10},{4,1},{5,9},{6,3},{7,11},{8,4},{9,12},{10... | collective-permute-start | bytes 1769480 | tf_op jit(solution)/shard_map/ppermute | solution.py:167
  39.6 6.8 %collective-permute-start.17 = (bf16[192,1792]{1,0:T(8,128)(2,1)}, bf16[192,1792]{1,0:T(8,128)(2,1)}, u32[]{:S(2)}, u32[]{:S(2)}) collective-permute-start(bf16[192,1792]{1,0:T(8,128)(2,1)} %pad_maximum_fusion.13), channel_id=1, source_target_pairs={{0,0},{1,1},{2,2},{3,3},{4,4},{5,5},{6,6},{7,7},{32,39},{33,32},{3... | collective-permute-start | bytes 2064392 | tf_op jit(solution)/shard_map/ppermute | solution.py:190
  88.5 6.1 %collective-permute-done.8 = bf16[64,1536]{0,1:T(8,128)(2,1)S(1)} collective-permute-done((bf16[64,1536]{0,1:T(8,128)(2,1)S(1)}, bf16[64,1536]{0,1:T(8,128)(2,1)S(1)}, u32[]{:S(2)}, u32[]{:S(2)}) %collective-permute-start.8) | collective-permute-done | bytes 196640 | tf_op jit(solution)/shard_map/ppermute | solution.py:46
  104.9 15.7 %collective-permute-start.27 = (bf16[64,1536]{1,0:T(8,128)(2,1)S(1)}, bf16[64,1536]{1,0:T(8,128)(2,1)S(1)}, u32[]{:S(2)}, u32[]{:S(2)}) collective-permute-start(bf16[64,1536]{1,0:T(8,128)(2,1)S(1)} %slice.498), channel_id=1, source_target_pairs={{0,3},{1,0},{2,1},{3,2},{4,7},{5,4},{6,5},{7,6},{8,11},{9,8},{10,9... | collective-permute-start | bytes 589832 | tf_op jit(solution)/shard_map/ppermute | solution.py:50
  147.3 5.7 %collective-permute-start.16 = (bf16[512,1664]{0,1:T(8,128)(2,1)}, bf16[512,1664]{0,1:T(8,128)(2,1)}, u32[]{:S(2)}, u32[]{:S(2)}) collective-permute-start(bf16[512,1664]{0,1:T(8,128)(2,1)} %concatenate.165), channel_id=1, source_target_pairs={{0,8},{8,0},{1,9},{9,1},{2,10},{10,2},{3,11},{11,3},{4,12},{12,4},... | collective-permute-start | bytes 5111816 | tf_op jit(solution)/shard_map/ppermute | solution.py:95
  154.4 8.7 %collective-permute-done.18 = bf16[128,1536]{1,0:T(8,128)(2,1)S(1)} collective-permute-done((bf16[128,1536]{1,0:T(8,128)(2,1)S(1)}, bf16[128,1536]{1,0:T(8,128)(2,1)S(1)}, u32[]{:S(2)}, u32[]{:S(2)}) %collective-permute-start.18) | collective-permute-done | bytes 393248 | tf_op jit(solution)/shard_map/ppermute | solution.py:201
  165.8 6.6 %concatenate.166 = bf16[1024,1664]{0,1:T(8,128)(2,1)} concatenate(bf16[128,1664]{0,1:T(8,128)(2,1)S(1)} %maximum_maximum_fusion.3, bf16[128,1664]{0,1:T(8,128)(2,1)S(1)} %collective-permute-done.12, bf16[128,1664]{0,1:T(8,128)(2,1)S(1)} %collective-permute-done.13, bf16[64,1664]{0,1:T(8,128)(2,1)S(1)} %collective-permute-done.14, bf16[64,1664]{0,1:T(8,128)(2,1)S(1)} %collective-permute-done.15, ...), dimensions={0} | concatenate | bytes 6815744 | tf_op jit(solution)/shard_map/concatenate | solution.py:257
  208.4 5.6 convolution_convert_fusion
  223.7 6.6 %convolution_convert_fusion.2 = bf16[1024,1536]{0,1:T(8,128)(2,1)S(1)} fusion(bf16[1536,1280]{1,0:T(8,128)(2,1)} %bitcast.261, bf16[1024,128]{1,0:T(8,128)(2,1)S(1)} %copy-done.44, bf16[1024,128]{1,0:T(8,128)(2,1)S(1)} %copy-done.43, bf16[1024,512]{1,0:T(8,128)(2,1)S(1)} %copy-done.37, bf16[1024,512]{1,0:T(8,128)(2,1)S(1)} %copy-done.36), kind=kOutput, calls=%fused_computation.19 | convolution fusion | flops 4038590464 | bytes 9699328 | tf_op jit(solution)/shard_map/dot_general | solution.py:34
  251.9 8.8 %collective-permute-done.30 = bf16[64,1664]{0,1:T(8,128)(2,1)S(1)} collective-permute-done((bf16[64,1664]{0,1:T(8,128)(2,1)S(1)}, bf16[64,1664]{0,1:T(8,128)(2,1)S(1)}, u32[]{:S(2)}, u32[]{:S(2)}) %collective-permute-start.30) | collective-permute-done | bytes 213024 | tf_op jit(solution)/shard_map/ppermute | solution.py:46
  267.4 4.8 collective-permute-done.33
  287.7 6.3 %collective-permute-done.35 = bf16[128,1536]{0,1:T(8,128)(2,1)S(1)} collective-permute-done((bf16[128,1536]{0,1:T(8,128)(2,1)S(1)}, bf16[128,1536]{0,1:T(8,128)(2,1)S(1)}, u32[]{:S(2)}, u32[]{:S(2)}) %collective-permute-start.35) | collective-permute-done | bytes 393248 | tf_op jit(solution)/shard_map/ppermute | solution.py:50
  295.8 6.2 %collective-permute-done.37 = bf16[64,1536]{0,1:T(8,128)(2,1)S(1)} collective-permute-done((bf16[64,1536]{0,1:T(8,128)(2,1)S(1)}, bf16[64,1536]{0,1:T(8,128)(2,1)S(1)}, u32[]{:S(2)}, u32[]{:S(2)}) %collective-permute-start.37) | collective-permute-done | bytes 196640 | tf_op jit(solution)/shard_map/ppermute | solution.py:50
  325.7 5.7 %all-to-all-start.4 = ((bf16[4,16,768]{2,1,0:T(8,128)(2,1)}), bf16[4,16,768]{2,1,0:T(8,128)(2,1)S(1)}, u32[]{:S(2)}, u32[]{:S(2)}) async-start(bf16[4,16,768]{2,1,0:T(8,128)(2,1)} %bitcast_select_fusion), calls=%async_computation.5 | async-start | bytes 196608 | tf_op jit(solution)/shard_map/all_to_all | solution.py:42
  339.9 4.8 fusion.8
  354.5 5.8 %reshape.385 = bf16[8,8,24,2,384]{4,3,2,1,0:T(2,128)(2,1)} reshape(bf16[1536,768]{1,0:T(8,128)(2,1)} %copy.309) | data formatting | bytes 4718592 | tf_op jit(solution)/shard_map/reshape | solution.py:370
  363.8 6.4 %collective-permute-start.43 = (bf16[8,288,384]{2,1,0:T(8,128)(2,1)}, bf16[8,288,384]{2,1,0:T(8,128)(2,1)}, u32[]{:S(2)}, u32[]{:S(2)}) collective-permute-start(bf16[8,288,384]{2,1,0:T(8,128)(2,1)} %fusion.19), channel_id=1, source_target_pairs={{0,8},{8,0},{1,9},{9,1},{2,10},{10,2},{3,11},{11,3},{4,12},{12,4},... | collective-permute-start | bytes 5308424 | tf_op jit(solution)/shard_map/ppermute | solution.py:95
  377.0 22.1 %all-to-all-start.1 = ((bf16[8,288,384]{2,1,0:T(8,128)(2,1)}), bf16[8,288,384]{2,1,0:T(8,128)(2,1)S(1)}, u32[]{:S(2)}, u32[]{:S(2)}) async-start(bf16[8,288,384]{2,1,0:T(8,128)(2,1)} %fusion.6), calls=%async_computation.1 | async-start | bytes 3538944 | tf_op jit(solution)/shard_map/all_to_all | solution.py:42
  407.3 47.3 %all-to-all-done.1 = bf16[8,288,384]{2,1,0:T(8,128)(2,1)S(1)} async-done(((bf16[8,288,384]{2,1,0:T(8,128)(2,1)}), bf16[8,288,384]{2,1,0:T(8,128)(2,1)S(1)}, u32[]{:S(2)}, u32[]{:S(2)}) %all-to-all-start.1) | async-done | bytes 1769504 | tf_op jit(solution)/shard_map/all_to_all | solution.py:42
  458.5 4.8 all-to-all-start.2
  469.2 7.9 %all-to-all-done.2 = bf16[16,72,384]{2,1,0:T(8,128)(2,1)S(1)} async-done(((bf16[16,72,384]{2,1,0:T(8,128)(2,1)}), bf16[16,72,384]{2,1,0:T(8,128)(2,1)S(1)}, u32[]{:S(2)}, u32[]{:S(2)}) %all-to-all-start.2) | async-done | bytes 884768 | tf_op jit(solution)/shard_map/all_to_all | solution.py:42
  502.4 8.2 %collective-permute-start.52 = (bf16[8,144,384]{2,1,0:T(8,128)(2,1)S(1)}, bf16[8,144,384]{2,1,0:T(8,128)(2,1)}, u32[]{:S(2)}, u32[]{:S(2)}) collective-permute-start(bf16[8,144,384]{2,1,0:T(8,128)(2,1)S(1)} %bitcast_dynamic-update-slice_fusion.6), channel_id=1, source_target_pairs={{0,8},{8,0},{1,9},{9,1},{2,10},{10,2},{3,11},{11,3},{4,12},{12,4},... | collective-permute-start | bytes 2654216 | tf_op jit(solution)/shard_map/ppermute | solution.py:95
  553.2 6.3 %copy.331 = f32[8,24,8,1024]{3,2,1,0:T(8,128)} copy(f32[8,24,8,1024]{3,1,2,0:T(8,128)S(1)} %convert_bitcast_fusion) | data formatting | bytes 12582912 | tf_op jit(solution)/shard_map/convert_element_type | solution.py:327
  (508 shorter events, 330.1 us)
Async XLA Ops:
  7.2 40.1 %collective-permute-start = (bf16[128,1536]{1,0:T(8,128)(2,1)}, bf16[128,1536]{1,0:T(8,128)(2,1)}, u32[]{:S(2)}, u32[]{:S(2)}) collective-permute-start(bf16[128,1536]{1,0:T(8,128)(2,1)} %param.16), channel_id=1, source_target_pairs={{0,1},{1,2},{2,3},{3,0},{4,5},{5,6},{6,7},{7,4},{8,9},{9,10},{10,1... | collective-permute-start | bytes 1179656 | tf_op jit(solution)/shard_map/ppermute | solution.py:46
  9.3 39.0 %collective-permute-start.1 = (bf16[128,1536]{1,0:T(8,128)(2,1)}, bf16[128,1536]{1,0:T(8,128)(2,1)}, u32[]{:S(2)}, u32[]{:S(2)}) collective-permute-start(bf16[128,1536]{1,0:T(8,128)(2,1)} %param.16), channel_id=1, source_target_pairs={{0,3},{1,0},{2,1},{3,2},{4,7},{5,4},{6,5},{7,6},{8,11},{9,8},{10,9... | collective-permute-start | bytes 1179656 | tf_op jit(solution)/shard_map/ppermute | solution.py:50
  20.3 36.1 %all-to-all-start = ((bf16[8,104,640]{2,1,0:T(8,128)(2,1)}), bf16[8,104,640]{2,1,0:T(8,128)(2,1)}, u32[]{:S(2)}, u32[]{:S(2)}) async-start(bf16[8,104,640]{2,1,0:T(8,128)(2,1)} %maximum_maximum_fusion.1), calls=%async_computation | async-start | bytes 2129920 | tf_op jit(solution)/shard_map/all_to_all | solution.py:42
  25.8 147.5 %all-gather.5.cloned.1.call-start = ((), (), s32[]{:S(2)}) async-start(), calls=%async_computation.7 | async-start | bytes 6193152 | tf_op jit(solution)/shard_map/all_gather | solution.py:195
  25.9 28.8 %collective-permute-start.6 = (bf16[192,1536]{1,0:T(8,128)(2,1)}, bf16[192,1536]{1,0:T(8,128)(2,1)}, u32[]{:S(2)}, u32[]{:S(2)}) collective-permute-start(bf16[192,1536]{1,0:T(8,128)(2,1)} %param.23), channel_id=1, source_target_pairs={{0,0},{1,8},{2,2},{3,10},{4,1},{5,9},{6,3},{7,11},{8,4},{9,12},{10... | collective-permute-start | bytes 1769480 | tf_op jit(solution)/shard_map/ppermute | solution.py:167
  39.6 20.0 %collective-permute-start.17 = (bf16[192,1792]{1,0:T(8,128)(2,1)}, bf16[192,1792]{1,0:T(8,128)(2,1)}, u32[]{:S(2)}, u32[]{:S(2)}) collective-permute-start(bf16[192,1792]{1,0:T(8,128)(2,1)} %pad_maximum_fusion.13), channel_id=1, source_target_pairs={{0,0},{1,1},{2,2},{3,3},{4,4},{5,5},{6,6},{7,7},{32,39},{33,32},{3... | collective-permute-start | bytes 2064392 | tf_op jit(solution)/shard_map/ppermute | solution.py:190
  59.6 264.5 %reduce-scatter.2.cloned.1.call-start = ((), (), s32[]{:S(2)}) async-start(), calls=%async_computation.6 | async-start | bytes 6709248 | tf_op jit(solution)/shard_map/reduce_scatter | solution.py:313
  85.8 17.2 %collective-permute-start.24 = (bf16[128,1536]{1,0:T(8,128)(2,1)}, bf16[128,1536]{1,0:T(8,128)(2,1)}, u32[]{:S(2)}, u32[]{:S(2)}) collective-permute-start(bf16[128,1536]{1,0:T(8,128)(2,1)} %param.30), channel_id=1, source_target_pairs={{0,1},{1,2},{2,3},{3,0},{4,5},{5,6},{6,7},{7,4},{8,9},{9,10},{10,1... | collective-permute-start | bytes 1179656 | tf_op jit(solution)/shard_map/ppermute | solution.py:46
  85.8 18.2 %collective-permute-start.25 = (bf16[128,1536]{1,0:T(8,128)(2,1)}, bf16[128,1536]{1,0:T(8,128)(2,1)}, u32[]{:S(2)}, u32[]{:S(2)}) collective-permute-start(bf16[128,1536]{1,0:T(8,128)(2,1)} %param.30), channel_id=1, source_target_pairs={{0,3},{1,0},{2,1},{3,2},{4,7},{5,4},{6,5},{7,6},{8,11},{9,8},{10,9... | collective-permute-start | bytes 1179656 | tf_op jit(solution)/shard_map/ppermute | solution.py:50
  95.8 28.5 %collective-permute-start.11 = (bf16[128,1536]{0,1:T(8,128)(2,1)}, bf16[128,1536]{0,1:T(8,128)(2,1)}, u32[]{:S(2)}, u32[]{:S(2)}) collective-permute-start(bf16[128,1536]{0,1:T(8,128)(2,1)} %pad_maximum_fusion.23), channel_id=1, source_target_pairs={{0,3},{1,0},{2,1},{3,2},{4,7},{5,4},{6,5},{7,6},{8,11},{9,8},{10,9... | collective-permute-start | bytes 1179656 | tf_op jit(solution)/shard_map/ppermute | solution.py:50
  98.5 25.9 %collective-permute-start.9 = (bf16[128,1536]{0,1:T(8,128)(2,1)S(1)}, bf16[128,1536]{0,1:T(8,128)(2,1)S(1)}, u32[]{:S(2)}, u32[]{:S(2)}) collective-permute-start(bf16[128,1536]{0,1:T(8,128)(2,1)S(1)} %pad_maximum_fusion.22), channel_id=1, source_target_pairs={{0,1},{1,2},{2,3},{3,0},{4,5},{5,6},{6,7},{7,4},{8,9},{9,10},{10,1... | collective-permute-start | bytes 1179656 | tf_op jit(solution)/shard_map/ppermute | solution.py:46
  103.9 27.1 %collective-permute-start.26 = (bf16[64,1536]{1,0:T(8,128)(2,1)S(1)}, bf16[64,1536]{1,0:T(8,128)(2,1)}, u32[]{:S(2)}, u32[]{:S(2)}) collective-permute-start(bf16[64,1536]{1,0:T(8,128)(2,1)S(1)} %slice.497), channel_id=1, source_target_pairs={{0,1},{1,2},{2,3},{3,0},{4,5},{5,6},{6,7},{7,4},{8,9},{9,10},{10,1... | collective-permute-start | bytes 589832 | tf_op jit(solution)/shard_map/ppermute | solution.py:46
  104.9 32.9 %collective-permute-start.27 = (bf16[64,1536]{1,0:T(8,128)(2,1)S(1)}, bf16[64,1536]{1,0:T(8,128)(2,1)S(1)}, u32[]{:S(2)}, u32[]{:S(2)}) collective-permute-start(bf16[64,1536]{1,0:T(8,128)(2,1)S(1)} %slice.498), channel_id=1, source_target_pairs={{0,3},{1,0},{2,1},{3,2},{4,7},{5,4},{6,5},{7,6},{8,11},{9,8},{10,9... | collective-permute-start | bytes 589832 | tf_op jit(solution)/shard_map/ppermute | solution.py:50
  138.6 24.6 %collective-permute-start.28 = (bf16[512,1536]{1,0:T(8,128)(2,1)}, bf16[512,1536]{1,0:T(8,128)(2,1)}, u32[]{:S(2)}, u32[]{:S(2)}) collective-permute-start(bf16[512,1536]{1,0:T(8,128)(2,1)} %get-tuple-element.179), channel_id=1, source_target_pairs={{0,8},{8,0},{1,9},{9,1},{2,10},{10,2},{3,11},{11,3},{4,12},{12,4},... | collective-permute-start | bytes 4718600 | tf_op jit(solution)/shard_map/ppermute | solution.py:95
  147.3 18.6 %collective-permute-start.16 = (bf16[512,1664]{0,1:T(8,128)(2,1)}, bf16[512,1664]{0,1:T(8,128)(2,1)}, u32[]{:S(2)}, u32[]{:S(2)}) collective-permute-start(bf16[512,1664]{0,1:T(8,128)(2,1)} %concatenate.165), channel_id=1, source_target_pairs={{0,8},{8,0},{1,9},{9,1},{2,10},{10,2},{3,11},{11,3},{4,12},{12,4},... | collective-permute-start | bytes 5111816 | tf_op jit(solution)/shard_map/ppermute | solution.py:95
  264.4 16.2 %collective-permute-start.23 = (bf16[128,1536]{0,1:T(8,128)(2,1)S(1)}, bf16[128,1536]{0,1:T(8,128)(2,1)S(1)}, u32[]{:S(2)}, u32[]{:S(2)}) collective-permute-start(bf16[128,1536]{0,1:T(8,128)(2,1)S(1)} %pad_maximum_fusion.25), channel_id=1, source_target_pairs={{0,3},{1,0},{2,1},{3,2},{4,7},{5,4},{6,5},{7,6},{8,11},{9,8},{10,9... | collective-permute-start | bytes 1179656 | tf_op jit(solution)/shard_map/ppermute | solution.py:50
  267.3 16.6 %collective-permute-start.21 = (bf16[128,1536]{0,1:T(8,128)(2,1)S(1)}, bf16[128,1536]{0,1:T(8,128)(2,1)S(1)}, u32[]{:S(2)}, u32[]{:S(2)}) collective-permute-start(bf16[128,1536]{0,1:T(8,128)(2,1)S(1)} %pad_maximum_fusion.24), channel_id=1, source_target_pairs={{0,1},{1,2},{2,3},{3,0},{4,5},{5,6},{6,7},{7,4},{8,9},{9,10},{10,1... | collective-permute-start | bytes 1179656 | tf_op jit(solution)/shard_map/ppermute | solution.py:46
  339.4 191.5 %all-gather.7.cloned.1.call-start = ((), (), s32[]{:S(2)}) async-start(), calls=%async_computation.8 | async-start | bytes 6623232 | tf_op jit(solution)/shard_map/all_gather | solution.py:322
  377.0 77.6 %all-to-all-start.1 = ((bf16[8,288,384]{2,1,0:T(8,128)(2,1)}), bf16[8,288,384]{2,1,0:T(8,128)(2,1)S(1)}, u32[]{:S(2)}, u32[]{:S(2)}) async-start(bf16[8,288,384]{2,1,0:T(8,128)(2,1)} %fusion.6), calls=%async_computation.1 | async-start | bytes 3538944 | tf_op jit(solution)/shard_map/all_to_all | solution.py:42
  404.6 58.6 %collective-permute-start.39 = (bf16[64,1536]{0,1:T(8,128)(2,1)}, bf16[64,1536]{0,1:T(8,128)(2,1)}, u32[]{:S(2)}, u32[]{:S(2)}) collective-permute-start(bf16[64,1536]{0,1:T(8,128)(2,1)} %get-tuple-element.137), channel_id=1, source_target_pairs={{0,1},{1,2},{2,3},{3,0},{4,5},{5,6},{6,7},{7,4},{8,9},{9,10},{10,1... | collective-permute-start | bytes 589832 | tf_op jit(solution)/shard_map/ppermute | solution.py:46
  405.1 58.2 %collective-permute-start.41 = (bf16[64,1536]{0,1:T(8,128)(2,1)}, bf16[64,1536]{0,1:T(8,128)(2,1)}, u32[]{:S(2)}, u32[]{:S(2)}) collective-permute-start(bf16[64,1536]{0,1:T(8,128)(2,1)} %get-tuple-element.138), channel_id=1, source_target_pairs={{0,3},{1,0},{2,1},{3,2},{4,7},{5,4},{6,5},{7,6},{8,11},{9,8},{10,9... | collective-permute-start | bytes 589832 | tf_op jit(solution)/shard_map/ppermute | solution.py:50
  458.5 18.6 %all-to-all-start.2 = ((bf16[16,72,384]{2,1,0:T(8,128)(2,1)}), bf16[16,72,384]{2,1,0:T(8,128)(2,1)S(1)}, u32[]{:S(2)}, u32[]{:S(2)}) async-start(bf16[16,72,384]{2,1,0:T(8,128)(2,1)} %maximum_maximum_fusion.2), calls=%async_computation.2 | async-start | bytes 1769472 | tf_op jit(solution)/shard_map/all_to_all | solution.py:42
  465.7 44.9 %collective-permute-start.42 = (bf16[128,1536]{0,1:T(8,128)(2,1)}, bf16[128,1536]{0,1:T(8,128)(2,1)}, u32[]{:S(2)}, u32[]{:S(2)}) collective-permute-start(bf16[128,1536]{0,1:T(8,128)(2,1)} %pad_maximum_fusion.27), channel_id=1, source_target_pairs={{0,3},{1,0},{2,1},{3,2},{4,7},{5,4},{6,5},{7,6},{8,11},{9,8},{10,9... | collective-permute-start | bytes 1179656 | tf_op jit(solution)/shard_map/ppermute | solution.py:50
  469.2 41.4 %collective-permute-start.40 = (bf16[128,1536]{0,1:T(8,128)(2,1)}, bf16[128,1536]{0,1:T(8,128)(2,1)}, u32[]{:S(2)}, u32[]{:S(2)}) collective-permute-start(bf16[128,1536]{0,1:T(8,128)(2,1)} %pad_maximum_fusion.26), channel_id=1, source_target_pairs={{0,1},{1,2},{2,3},{3,0},{4,5},{5,6},{6,7},{7,4},{8,9},{9,10},{10,1... | collective-permute-start | bytes 1179656 | tf_op jit(solution)/shard_map/ppermute | solution.py:46
  (115 other events, 1045.9 us)
Sparse Core Ops, SparseCore 0:
  59.7 82.8 all-gather.4
  219.6 87.4 reduce-scatter.1
  350.2 127.3 all-gather.6
